TPU v7x, 256 devices: a whole 4x4x8 slice. The times are simulated.
256 devices in a mesh: seq: 32 (over y, z_lo, core), mp: 8 (over x, z_hi).
Axes of the slice: x: 4, y: 4, z: 8 (z_hi: 2, z_lo: 4; z = z_hi * 4 + z_lo), core: 2. Of those that a mesh axis runs over, the one named last changes fastest.
Arguments:
- query: bfloat16 [24576, 4096], P('seq', 'mp'), may hold values from -5 to 5
- key: bfloat16 [24576, 4096], P('seq', 'mp'), may hold values from -5 to 5
- value: bfloat16 [24576, 4096], P('seq', 'mp'), may hold values from -6 to 6
- weight_out: bfloat16 [4096, 4096], P('mp', 'seq'), may hold values from -0.09375 to 0.09375
- output_gradient: bfloat16 [24576, 4096], P('seq', 'mp'), may hold values from -6 to 6
Outputs:
- output: bfloat16 [24576, 4096], P('seq', 'mp')
- grad_query: bfloat16 [24576, 4096], P('seq', 'mp')
- grad_key: bfloat16 [24576, 4096], P('seq', 'mp')
- grad_value: bfloat16 [24576, 4096], P('seq', 'mp')
- grad_weight: bfloat16 [4096, 4096], P('mp', 'seq')
All inputs are finite; a program needn't handle non-finite values.
Results may differ from a plain program's by a relative error of at most 0.03.
Values may be sent and summed in bfloat16 or wider, within the bound.
A program may use at most 128 MiB of HBM per device.

v0:
```python
import jax
import jax.numpy as jnp
from jax import lax
from jax.sharding import PartitionSpec as P

HEAD_WIDTH = 128
ROW_LENGTH = 256


def shifted(value, axis, steps):
    count = lax.axis_size(axis)
    initial, last = (max(0, -steps), min(count, count - steps))
    return lax.ppermute(value, axis, [(source, source + steps) for source in range(initial, last)])


def attend(queries, keys, values, grad_out, permitted_mask, factor):
    scores = (
        jnp.einsum("bqhe,bkhe->bhqk", queries, keys, preferred_element_type=jnp.float32) * factor
    )
    scores = jnp.where(permitted_mask, scores, -1e30)
    highest = jnp.max(scores, axis=-1, keepdims=True)
    weights = jnp.exp(scores - highest)
    probs = (weights / jnp.sum(weights, axis=-1, keepdims=True)).astype(jnp.bfloat16)
    outputs = jnp.einsum(
        "bhqk,bkhe->bqhe", probs, values, preferred_element_type=jnp.float32
    ).astype(jnp.bfloat16)
    grad_probs = jnp.einsum("bqhe,bkhe->bhqk", grad_out, values, preferred_element_type=jnp.float32)
    centre = jnp.einsum("bqhe,bqhe->bhq", grad_out, outputs, preferred_element_type=jnp.float32)[
        ..., None
    ]
    grad_scores = (probs.astype(jnp.float32) * (grad_probs - centre)).astype(jnp.bfloat16)
    grad_queries = (
        jnp.einsum("bhqk,bkhe->bqhe", grad_scores, keys, preferred_element_type=jnp.float32)
        * factor
    )
    grad_keys = (
        jnp.einsum("bhqk,bqhe->bkhe", grad_scores, queries, preferred_element_type=jnp.float32)
        * factor
    )
    grad_values = jnp.einsum("bhqk,bqhe->bkhe", probs, grad_out, preferred_element_type=jnp.float32)
    return (outputs, grad_queries, grad_keys, grad_values)


def per_device(query, key, value, weight_out, output_gradient):
    token_stream = query.shape[0]
    features = query.shape[1]
    half_width = features // 2
    head_halves = half_width // HEAD_WIDTH
    local_rows = token_stream // ROW_LENGTH
    sequence_count = lax.axis_size("seq")
    all_rows = local_rows * sequence_count
    column_width = ROW_LENGTH // sequence_count
    factor = HEAD_WIDTH ** (-0.5)
    contract_last = (((1,), (1,)), ((), ()))
    weight_rows = lax.all_gather(weight_out, "seq", axis=1, tiled=True)
    grad_full = lax.all_gather(output_gradient, "mp", axis=1, tiled=True)
    grad_wide = lax.dot_general(
        grad_full, weight_rows, contract_last, preferred_element_type=jnp.float32
    )
    grad_mixed = grad_wide.astype(jnp.bfloat16)

    def rows_of(input_tensor):
        return input_tensor[:, :half_width].reshape(local_rows, ROW_LENGTH, head_halves, HEAD_WIDTH)

    def cols_of(input_tensor):
        return input_tensor[:, half_width:].reshape(local_rows, ROW_LENGTH, half_width)

    packed = jnp.stack([cols_of(query), cols_of(key), cols_of(value), cols_of(grad_mixed)])
    arrived = lax.all_to_all(packed, "seq", split_axis=2, concat_axis=1, tiled=True)
    row_query = rows_of(query)
    row_key = rows_of(key)
    row_value = rows_of(value)
    row_grad = rows_of(grad_mixed)
    token_position = jnp.arange(ROW_LENGTH)[:, None]
    target_index = jnp.arange(2 * ROW_LENGTH)[None, :]
    attention_window = (target_index > token_position) & (
        target_index <= token_position + ROW_LENGTH
    )
    border_rows = jnp.stack(
        [
            key[token_stream - ROW_LENGTH :, :half_width],
            value[token_stream - ROW_LENGTH :, :half_width],
        ]
    )
    prior_rows = shifted(border_rows, "seq", 1).reshape(2, ROW_LENGTH, head_halves, HEAD_WIDTH)
    row_keys = jnp.concatenate(
        [jnp.concatenate([prior_rows[0][None], row_key[:-1]], axis=0), row_key], axis=1
    )
    row_values = jnp.concatenate(
        [jnp.concatenate([prior_rows[1][None], row_value[:-1]], axis=0), row_value], axis=1
    )
    initial_window = (jnp.arange(local_rows) == 0) & (lax.axis_index("seq") == 0)
    permitted_mask = attention_window[None, None] & (
        (target_index >= ROW_LENGTH)[None, None]
        | jnp.logical_not(initial_window)[:, None, None, None]
    )
    row_out, row_gquery, row_key_gradient, row_value_gradient = attend(
        row_query, row_keys, row_values, row_grad, permitted_mask, factor
    )

    def settle_local(value_portion):
        subsequent_rows = jnp.concatenate(
            [value_portion[1:, :ROW_LENGTH], jnp.zeros_like(value_portion[:1, :ROW_LENGTH])], axis=0
        )
        return value_portion[:, ROW_LENGTH:] + subsequent_rows

    own_key = settle_local(row_key_gradient)
    own_value = settle_local(row_value_gradient)
    return_block = jnp.stack(
        [row_key_gradient[0, :ROW_LENGTH], row_value_gradient[0, :ROW_LENGTH]]
    ).reshape(2, ROW_LENGTH, half_width)
    incoming_block = (
        shifted(return_block.astype(jnp.bfloat16), "seq", -1)
        .astype(return_block.dtype)
        .reshape(2, ROW_LENGTH, head_halves, HEAD_WIDTH)
    )
    extra_key = incoming_block[0]
    extra_value = incoming_block[1]
    own_key = jnp.concatenate([own_key[:-1], own_key[-1:] + extra_key[None]], axis=0)
    own_value = jnp.concatenate([own_value[:-1], own_value[-1:] + extra_value[None]], axis=0)
    position_lattice = arrived.reshape(
        4, all_rows, column_width, head_halves, HEAD_WIDTH
    ).transpose(0, 2, 1, 3, 4)
    causal = jnp.arange(all_rows)[:, None] >= jnp.arange(all_rows)[None, :]
    col_out, col_gquery, col_gkey, col_gvalue = attend(
        position_lattice[0],
        position_lattice[1],
        position_lattice[2],
        position_lattice[3],
        causal[None, None],
        factor,
    )
    results = jnp.stack(
        [
            col_out,
            col_gquery.astype(jnp.bfloat16),
            col_gkey.astype(jnp.bfloat16),
            col_gvalue.astype(jnp.bfloat16),
        ]
    )
    results = results.transpose(0, 2, 1, 3, 4).reshape(4, all_rows, column_width, half_width)
    returned = lax.all_to_all(results, "seq", split_axis=1, concat_axis=2, tiled=True).reshape(
        4, token_stream, half_width
    )

    def join(row_portion, column_portion):
        return jnp.concatenate(
            [row_portion.reshape(token_stream, half_width), column_portion], axis=1
        )

    mixed = join(row_out, returned[0])
    grad_query = join(row_gquery.astype(jnp.bfloat16), returned[1])
    grad_key = join(own_key.astype(jnp.bfloat16), returned[2])
    grad_value = join(own_value.astype(jnp.bfloat16), returned[3])
    value_portion = jnp.dot(mixed, weight_rows, preferred_element_type=jnp.float32)
    output = lax.psum_scatter(
        value_portion.astype(jnp.bfloat16), "mp", scatter_dimension=1, tiled=True
    )
    summed = lax.psum_scatter(
        lax.dot_general(
            grad_full, mixed, (((0,), (0,)), ((), ())), preferred_element_type=jnp.float32
        ).astype(jnp.bfloat16),
        "seq",
        scatter_dimension=0,
        tiled=True,
    ).astype(jnp.float32)
    grad_weight = summed.T.astype(jnp.bfloat16)
    return (output, grad_query, grad_key, grad_value, grad_weight)


def solution(mesh):
    in_specs = (P("seq", "mp"), P("seq", "mp"), P("seq", "mp"), P("mp", "seq"), P("seq", "mp"))
    out_specs = (P("seq", "mp"), P("seq", "mp"), P("seq", "mp"), P("seq", "mp"), P("mp", "seq"))
    return jax.shard_map(
        per_device, mesh=mesh, in_specs=in_specs, out_specs=out_specs, check_vma=False
    )
```

profile of v0, /device:TPU:96, one launch (start us, length us, event | category | flops | bytes accessed | tf_op | source)
XLA Modules:
  0.0 679.3 jit_solution(14203803032662883171)
XLA Ops:
  7.2 0.7 all-gather.5.cloned.1.call-update
  8.0 0.7 all-gather.3.cloned.1.call-update
  8.7 2.0 fusion.40
  10.7 0.8 fusion.39
  11.5 0.8 fusion.38
  12.2 69.5 %all-gather.5.cloned.1.call-done = bf16[512,4096]{1,0:T(8,128)(2,1)} async-done(((bf16[512,128]{1,0:T(8,128)(2,1)}), bf16[512,4096]{1,0:T(8,128)(2,1)}) %all-gather.5.cloned.1.call-update) | async-done | bytes 4194320 | tf_op jit(solution)/shard_map/all_gather | solution.py:55
  81.8 142.4 %all-gather.3.cloned.1.call-done = bf16[768,4096]{1,0:T(8,128)(2,1)} async-done(((bf16[768,512]{1,0:T(8,128)(2,1)}), bf16[768,4096]{1,0:T(8,128)(2,1)}) %all-gather.3.cloned.1.call-update) | async-done | bytes 6291472 | tf_op jit(solution)/shard_map/all_gather | solution.py:56
  224.2 7.4 %convolution_convert_fusion.2 = bf16[768,512]{1,0:T(8,128)(2,1)S(1)} fusion(bf16[768,4096]{1,0:T(8,128)(2,1)} %all-gather.3.cloned.1.call-done, bf16[512,4096]{1,0:T(8,128)(2,1)} %all-gather.5.cloned.1.call-done), kind=kOutput, calls=%fused_computation.21 | convolution fusion | flops 3221618688 | bytes 11272192 | tf_op jit(solution)/shard_map/dot_general | solution.py:57
  231.6 0.8 fusion.37
  232.6 2.4 copy.166
  235.1 12.4 %all-to-all-start = ((bf16[4,3,256,256]{3,0,1,2:T(4,128)(2,1)}), bf16[4,3,256,256]{3,0,1,2:T(4,128)(2,1)S(1)}, u32[]{:S(2)}, u32[]{:S(2)}) async-start(bf16[4,3,256,256]{3,0,1,2:T(4,128)(2,1)} %copy.166), calls=%async_computation | async-start | bytes 3145728 | tf_op jit(solution)/shard_map/all_to_all | solution.py:69
  247.5 0.8 copy.217
  248.3 0.8 copy.218
  249.1 33.5 %all-to-all-done = bf16[4,3,256,256]{3,0,1,2:T(4,128)(2,1)S(1)} async-done(((bf16[4,3,256,256]{3,0,1,2:T(4,128)(2,1)}), bf16[4,3,256,256]{3,0,1,2:T(4,128)(2,1)S(1)}, u32[]{:S(2)}, u32[]{:S(2)}) %all-to-all-start) | async-done | bytes 1572896 | tf_op jit(solution)/shard_map/all_to_all | solution.py:69
  283.4 1.3 fusion.43
  284.7 1.2 divide_convert_fusion.1
  285.9 0.6 fusion.19
  287.9 1.0 copy.230
  288.9 1.5 copy.174
  290.4 8.1 %all-to-all-start.1 = ((bf16[4,96,8,256]{3,2,0,1:T(8,128)(2,1)}), bf16[4,96,8,256]{3,2,0,1:T(8,128)(2,1)S(1)}, u32[]{:S(2)}, u32[]{:S(2)}) async-start(bf16[4,96,8,256]{3,2,0,1:T(8,128)(2,1)} %copy.174), calls=%async_computation.1 | async-start | bytes 3145728 | tf_op jit(solution)/shard_map/all_to_all | solution.py:142
  298.6 0.7 pad_maximum_fusion.15
  299.3 2.2 collective-permute-start
  301.6 0.7 fusion.20
  302.4 0.7 slice.139
  303.1 0.7 slice.134
  303.8 1.1 reshape.165
  305.0 1.3 reshape.166
  306.3 0.4 copy.185
  306.7 1.0 slice.140
  307.8 0.7 copy.161
  308.6 1.0 copy.159
  309.7 0.9 copy.158
  310.6 1.0 broadcast_and_fusion
  311.6 12.6 %collective-permute-done = bf16[2,256,256]{1,2,0:T(8,128)(2,1)} collective-permute-done((bf16[2,256,256]{1,2,0:T(8,128)(2,1)}, bf16[2,256,256]{1,2,0:T(8,128)(2,1)}, u32[]{:S(2)}, u32[]{:S(2)}) %collective-permute-start) | collective-permute-done | bytes 262176 | tf_op jit(solution)/shard_map/ppermute | solution.py:13
  324.2 1.6 fusion.42
  326.0 0.6 fusion.23
  327.1 1.8 fusion.44
  329.1 1.8 reshape.170
  330.9 2.1 bitcast_convert_fusion
  333.1 2.1 copy.209
  335.2 2.5 multiply_reduce_fusion
  337.7 2.0 copy.165
  339.7 1.8 copy.236
  341.6 1.0 fusion.36
  342.7 7.9 %fusion.2 = bf16[4096,512]{0,1:T(8,128)(2,1)} fusion(bf16[768,4096]{1,0:T(8,128)(2,1)} %all-gather.3.cloned.1.call-done, bf16[768,256]{1,0:T(8,128)(2,1)S(1)} %bitcast.171, bf16[768,256]{1,0:T(8,128)(2,1)S(1)} %bitcast.169), kind=kOutput, calls=%fused_computation.4 | convolution fusion | flops 3224895488 | bytes 11272192 | tf_op jit(solution)/shard_map/dot_general | solution.py:160
  350.6 6.5 copy.215
  357.2 7.5 %convolution_convert_fusion = bf16[768,4096]{1,0:T(8,128)(2,1)} fusion(bf16[512,4096]{1,0:T(8,128)(2,1)} %all-gather.5.cloned.1.call-done, bf16[768,256]{1,0:T(8,128)(2,1)S(1)} %bitcast.172, bf16[768,256]{1,0:T(8,128)(2,1)S(1)} %bitcast.170), kind=kOutput, calls=%fused_computation.2 | convolution fusion | flops 3225944064 | bytes 11272192 | tf_op jit(solution)/shard_map/dot_general | solution.py:155
  364.7 1.0 copy-done
  365.7 1.0 copy.186
  366.7 1.7 convolution_bitcast_fusion
  368.6 0.7 multiply_convert_fusion
  369.3 0.6 multiply_bitcast_fusion
  370.1 1.9 collective-permute-start.1
  372.4 0.8 copy-done.9
  373.2 0.5 fusion.18
  373.7 0.4 copy.182
  374.2 2.2 collective-permute-done.1
  376.5 0.4 copy.190
  377.2 0.4 copy.188
  378.3 0.9 pad_maximum_fusion.6
  379.3 1.3 pad_maximum_fusion.4
  380.5 122.8 %reduce-scatter.7.cloned.1.call-done = bf16[128,512]{1,0:T(8,128)(2,1)} async-done(((bf16[4096,512]{1,0:T(8,128)(2,1)}), bf16[128,512]{1,0:T(8,128)(2,1)}) %reduce-scatter.7.cloned.1.call-update) | async-done | bytes 131088
  503.3 1.7 copy.216
  505.0 167.8 %reduce-scatter.5.cloned.1.call-done = bf16[768,512]{1,0:T(8,128)(2,1)} async-done(((bf16[768,4096]{1,0:T(8,128)(2,1)}), bf16[768,512]{1,0:T(8,128)(2,1)}) %reduce-scatter.5.cloned.1.call-update) | async-done | bytes 786448 | tf_op jit(solution)/shard_map/reduce_scatter | solution.py:156
  (94 shorter events, 5.6 us)
Async XLA Ops:
  7.2 3.5 copy-start.1
  7.2 74.6 %all-gather.5.cloned.1.call-start = ((), (), s32[]{:S(2)}) async-start(), calls=%async_computation.5 | async-start | bytes 4325376 | tf_op jit(solution)/shard_map/all_gather | solution.py:55
  7.9 216.3 %all-gather.3.cloned.1.call-start = ((), (), s32[]{:S(2)}) async-start(), calls=%async_computation.4 | async-start | bytes 7077888 | tf_op jit(solution)/shard_map/all_gather | solution.py:56
  8.7 2.8 copy-start.2
  235.1 47.6 %all-to-all-start = ((bf16[4,3,256,256]{3,0,1,2:T(4,128)(2,1)}), bf16[4,3,256,256]{3,0,1,2:T(4,128)(2,1)S(1)}, u32[]{:S(2)}, u32[]{:S(2)}) async-start(bf16[4,3,256,256]{3,0,1,2:T(4,128)(2,1)} %copy.166), calls=%async_computation | async-start | bytes 3145728 | tf_op jit(solution)/shard_map/all_to_all | solution.py:69
  290.4 8.2 %copy-start.15 = (bf16[256,256]{0,1:T(8,128)(2,1)S(1)}, bf16[256,256]{0,1:T(8,128)(2,1)}, u32[]{:S(2)}) copy-start(bf16[256,256]{0,1:T(8,128)(2,1)} %copy.217) | copy-start | bytes 393220
  290.4 8.2 %copy-start.16 = (bf16[256,256]{0,1:T(8,128)(2,1)S(1)}, bf16[256,256]{0,1:T(8,128)(2,1)}, u32[]{:S(2)}) copy-start(bf16[256,256]{0,1:T(8,128)(2,1)} %copy.218) | copy-start | bytes 393220
  290.4 51.1 %all-to-all-start.1 = ((bf16[4,96,8,256]{3,2,0,1:T(8,128)(2,1)}), bf16[4,96,8,256]{3,2,0,1:T(8,128)(2,1)S(1)}, u32[]{:S(2)}, u32[]{:S(2)}) async-start(bf16[4,96,8,256]{3,2,0,1:T(8,128)(2,1)} %copy.174), calls=%async_computation.1 | async-start | bytes 3145728 | tf_op jit(solution)/shard_map/all_to_all | solution.py:142
  298.5 204.8 %reduce-scatter.7.cloned.1.call-start = ((), (), s32[]{:S(2)}) async-start(), calls=%async_computation.7 | async-start | bytes 4325376
  299.3 24.9 %collective-permute-start = (bf16[2,256,256]{1,2,0:T(8,128)(2,1)}, bf16[2,256,256]{1,2,0:T(8,128)(2,1)}, u32[]{:S(2)}, u32[]{:S(2)}) collective-permute-start(bf16[2,256,256]{1,2,0:T(8,128)(2,1)} %pad_maximum_fusion.15), channel_id=1, source_target_pairs={{0,8},{8,16},{16,24},{24,32},{32,40},{40,48},{48,56},{56,64},{64,7... | collective-permute-start | bytes 786440 | tf_op jit(solution)/shard_map/ppermute | solution.py:13
  304.9 3.6 copy-start.7
  305.0 21.0 %copy-start.8 = (bf16[3,256,2,128]{3,1,2,0:T(8,128)(2,1)}, bf16[3,256,2,128]{3,1,2,0:T(8,128)(2,1)S(1)}, u32[]{:S(2)}) copy-start(bf16[3,256,2,128]{3,1,2,0:T(8,128)(2,1)S(1)} %copy.162) | copy-start | bytes 1179652
  306.3 3.4 copy-start.10
  307.8 2.8 copy-start.17
  308.6 17.4 %copy-start.11 = (bf16[2,256,2,128]{3,1,2,0:T(8,128)(2,1)S(1)}, bf16[2,256,2,128]{3,1,2,0:T(8,128)(2,1)}, u32[]{:S(2)}) copy-start(bf16[2,256,2,128]{3,1,2,0:T(8,128)(2,1)} %copy.161) | copy-start | bytes 786436
  326.0 0.7 copy-start.13
  326.0 1.0 copy-start.20
  341.6 1.2 copy-start.19
  357.1 315.6 %reduce-scatter.5.cloned.1.call-start = ((), (), s32[]{:S(2)}) async-start(), calls=%async_computation.6 | async-start | bytes 7077888 | tf_op jit(solution)/shard_map/reduce_scatter | solution.py:156
  364.7 1.0 copy-start
  366.7 1.8 copy-start.6
  366.7 1.8 copy-start.18
  366.7 1.8 copy-start.21
  366.7 1.8 copy-start.22
  370.1 6.3 collective-permute-start.1
  372.1 1.0 copy-start.9
  372.1 1.1 copy-start.12
  372.2 1.1 copy-start.14
  377.0 1.0 copy-start.5
  377.1 1.1 copy-start.4
  377.1 1.2 copy-start.3
Sparse Core Ops, SparseCore 0:
  9.8 71.9 all-gather.4
  84.2 139.8 all-gather.2
  357.2 146.0 reduce-scatter.6
  507.9 164.7 reduce-scatter.4
where the time goes:
time: 684 us; the launch traced here: 679 us
  waiting for transfers between devices  552 us (81%)
  local copies, waits for them, and re-layouts  44.3 us (6%)
  matrix products  32.5 us (5%)
  starting transfers between devices  24.8 us (4%)
  between operations  14.4 us (2%)
  other arithmetic  11 us (2%)
    reduce_scatter x1, waiting for transfers between devices, per_device(): lax.psum_scatter(value_portion.astype(jnp.bfloat16), 'mp', scatter_dimens...  168 us
    all_gather x1, waiting for transfers between devices, per_device(): grad_full = lax.all_gather(output_gradient, 'mp', axis=1, tiled=True)  142 us
    unnamed x5, waiting for transfers between devices  124 us
    all_gather x1, waiting for transfers between devices, per_device(): weight_rows = lax.all_gather(weight_out, 'seq', axis=1, tiled=True)  69.5 us
    all_to_all x1, waiting for transfers between devices, per_device(): lax.all_to_all(packed, 'seq', split_axis=2, concat_axis=1, tiled=True)  33.5 us
    unnamed x55, local copies, waits for them, and re-layouts  16.8 us
    ppermute x2, waiting for transfers between devices, shifted(): lax.ppermute(value, axis, [(source, source + steps) for source in range(i...  14.8 us
  transfers between devices with their start and end apart: 8, of which 7 were waited for; matrix products, arithmetic and copies ran while one was open for 7% of the time, Pallas kernels for 0%

commit v1 on v0

--- a/solution.py
+++ b/solution.py
@@ -1,10 +1,336 @@
 import jax
 import jax.numpy as jnp
 from jax import lax
+from jax.experimental import pallas as pl
+from jax.experimental.pallas import tpu as pltpu
 from jax.sharding import PartitionSpec as P
 
 HEAD_WIDTH = 128
 ROW_LENGTH = 256
+MESH = pl.DeviceIdType.MESH
+F32 = jnp.float32
+BF16 = jnp.bfloat16
+
+
+def coords():
+    s = lax.axis_index("seq")
+    m = lax.axis_index("mp")
+    return s // 8, (s // 2) % 4, s % 2, m // 2, m % 2
+
+
+def device(y, zl, c, x, zh):
+    return (y * 8 + zl * 2 + c, x * 2 + zh)
+
+
+def remote(src, dst, send, recv, target):
+    return pltpu.make_async_remote_copy(
+        src_ref=src, dst_ref=dst, send_sem=send, recv_sem=recv, device_id=target, device_id_type=MESH
+    )
+
+
+def arrive(ref, sem):
+    pltpu.make_async_copy(ref, ref, sem).wait()
+
+
+def greet(targets):
+    barrier = pltpu.get_barrier_semaphore()
+    for target in targets:
+        pl.semaphore_signal(barrier, inc=1, device_id=target, device_id_type=MESH)
+    pl.semaphore_wait(barrier, len(targets))
+
+
+def neighbours():
+    y, zl, c, x, zh = coords()
+    core = device(y, zl, 1 - c, x, zh)
+    lines = [device(y, (zl + d) % 4, c, x, zh) for d in (1, 2, 3)]
+    rings = [device((y + d) % 4, zl, c, x, zh) for d in (1, 2, 3)]
+    right = device(y, zl, c, (x + 1) % 4, zh)
+    left = device(y, zl, c, (x + 3) % 4, zh)
+    far = device(y, zl, c, x, 1 - zh)
+    return core, lines, rings, right, left, far
+
+
+def wide(index, width):
+    return pl.ds(pl.multiple_of(index * width, width), width)
+
+
+def gather_kernel(
+    w_ref, og_ref, w_out, og_out, gm_ref, w_buf, og_buf, own_sem, w_send, w_recv, o_send, o_recv, out_sem
+):
+    y, zl, c, x, zh = coords()
+    core, lines, rings, right, left, far = neighbours()
+    greet([core, *lines, *rings, right, left, far])
+
+    def w_at(yy, zz, cc):
+        return w_buf.at[:, wide(yy * 8 + zz * 2 + cc, 128)]
+
+    def og_at(xx, hh):
+        return og_buf.at[:, wide(xx * 2 + hh, 512)]
+
+    def og_half(xx, hh, half):
+        return og_buf.at[pl.ds(384 * half, 384), wide(xx * 2 + hh, 512)]
+
+    sends = []
+
+    def go(src, dst, send, recv, target):
+        copy = remote(src, dst, send, recv, target)
+        copy.start()
+        sends.append(copy)
+
+    x1, x2, x3 = (x + 1) % 4, (x + 2) % 4, (x + 3) % 4
+    go(og_ref, og_at(x, zh), o_send.at[0], o_recv.at[0], far)
+    go(og_ref, og_at(x, zh), o_send.at[1], o_recv.at[1], right)
+    go(og_ref, og_at(x, zh), o_send.at[2], o_recv.at[2], left)
+    for d in range(3):
+        go(w_ref, w_at(y, zl, c), w_send.at[d], w_recv.at[d], lines[d])
+    go(w_ref, w_at(y, zl, c), w_send.at[3], w_recv.at[3], core)
+    own_w = pltpu.make_async_copy(w_ref, w_at(y, zl, c), own_sem.at[0])
+    own_w.start()
+    own_og = pltpu.make_async_copy(og_ref, og_at(x, zh), own_sem.at[1])
+    own_og.start()
+    own_w.wait()
+    number = 4
+    for d in range(3):
+        arrive(w_at(y, (zl + 3 - d) % 4, c), w_recv.at[d])
+    for d in range(3):
+        for k in range(4):
+            zz = (zl + k) % 4
+            go(w_at(y, zz, c), w_at(y, zz, c), w_send.at[number], w_recv.at[number], rings[d])
+            number += 1
+    for k in range(1, 4):
+        zz = (zl + k) % 4
+        go(w_at(y, zz, c), w_at(y, zz, c), w_send.at[number], w_recv.at[number], core)
+        number += 1
+    arrive(og_at(x3, zh), o_recv.at[1])
+    go(og_half(x3, zh, 0), og_half(x3, zh, 0), o_send.at[3], o_recv.at[3], right)
+    arrive(og_at(x1, zh), o_recv.at[2])
+    go(og_half(x1, zh, 1), og_half(x1, zh, 1), o_send.at[4], o_recv.at[4], left)
+    arrive(og_at(x, 1 - zh), o_recv.at[0])
+    go(og_at(x, 1 - zh), og_at(x, 1 - zh), o_send.at[5], o_recv.at[5], right)
+    go(og_at(x, 1 - zh), og_at(x, 1 - zh), o_send.at[6], o_recv.at[6], left)
+    first = 4
+    for d in range(3):
+        for k in range(4):
+            block = w_at((y + 3 - d) % 4, (zl + k) % 4, c)
+            arrive(block, w_recv.at[first + 4 * d + k])
+            go(block, block, w_send.at[number], w_recv.at[number], core)
+            number += 1
+    arrive(og_at(x3, 1 - zh), o_recv.at[5])
+    go(og_half(x3, 1 - zh, 0), og_half(x3, 1 - zh, 0), o_send.at[7], o_recv.at[7], right)
+    arrive(og_at(x1, 1 - zh), o_recv.at[6])
+    go(og_half(x1, 1 - zh, 1), og_half(x1, 1 - zh, 1), o_send.at[8], o_recv.at[8], left)
+    arrive(w_at(y, zl, 1 - c), w_recv.at[3])
+    for k in range(1, 4):
+        arrive(w_at(y, (zl + k) % 4, 1 - c), w_recv.at[15 + k])
+    for d in range(3):
+        for k in range(4):
+            arrive(w_at((y + 3 - d) % 4, (zl + k) % 4, 1 - c), w_recv.at[19 + 4 * d + k])
+    copy_w = pltpu.make_async_copy(w_buf, w_out, out_sem.at[0])
+    copy_w.start()
+    own_og.wait()
+    arrive(og_half(x2, zh, 0), o_recv.at[3])
+    arrive(og_half(x2, zh, 1), o_recv.at[4])
+    arrive(og_half(x2, 1 - zh, 0), o_recv.at[7])
+    arrive(og_half(x2, 1 - zh, 1), o_recv.at[8])
+    copy_og = pltpu.make_async_copy(og_buf, og_out, out_sem.at[1])
+    copy_og.start()
+
+    @pl.loop(0, 3)
+    def _(tile):
+        rows = wide(tile, 256)
+        gm_ref[rows, :] = lax.dot_general(
+            og_buf[rows, :], w_buf[...], (((1,), (1,)), ((), ())), preferred_element_type=F32
+        ).astype(BF16)
+
+    for copy in sends:
+        copy.wait_send()
+    copy_w.wait()
+    copy_og.wait()
+
+
+def gather(weight_out, output_gradient):
+    any_space = pl.BlockSpec(memory_space=pl.ANY)
+    dma = pltpu.SemaphoreType.DMA
+    return pl.pallas_call(
+        gather_kernel,
+        out_shape=(
+            jax.ShapeDtypeStruct((512, 4096), BF16),
+            jax.ShapeDtypeStruct((768, 4096), BF16),
+            jax.ShapeDtypeStruct((768, 512), BF16),
+        ),
+        in_specs=[any_space, any_space],
+        out_specs=(any_space, any_space, pl.BlockSpec(memory_space=pltpu.VMEM)),
+        scratch_shapes=[
+            pltpu.VMEM((512, 4096), BF16),
+            pltpu.VMEM((768, 4096), BF16),
+            dma((2,)),
+            dma((31,)),
+            dma((31,)),
+            dma((9,)),
+            dma((9,)),
+            dma((2,)),
+        ],
+        compiler_params=pltpu.CompilerParams(
+            collective_id=0, has_side_effects=True, vmem_limit_bytes=56 * 2**20
+        ),
+    )(weight_out, output_gradient)
+
+
+def reduce_kernel(
+    mixed_ref, w_ref, og_ref, out_ref, gw_ref,
+    part, relay_l, relay_r, direct_l, direct_r, far_send, far_recv, total,
+    gw_part, gw_core, gw_sum, gw_ring, gw_line, gw_last,
+    x_send, x_recv, z_send, z_recv, g_send, g_recv,
+):
+    y, zl, c, x, zh = coords()
+    core, lines, rings, right, left, far = neighbours()
+    greet([core, *lines, *rings, right, left, far])
+    x1, x2, x3 = (x + 1) % 4, (x + 2) % 4, (x + 3) % 4
+    halves = (1 - zh, zh)
+    top, low = pl.ds(0, 384), pl.ds(384, 384)
+    sends = []
+
+    def go(src, dst, send, recv, target):
+        copy = remote(src, dst, send, recv, target)
+        copy.start()
+        sends.append(copy)
+
+    def chunk(xx, k):
+        return wide(xx * 2 + halves[k], 512)
+
+    def project(xx, k):
+        columns = chunk(xx, k)
+
+        @pl.loop(0, 3)
+        def _(tile):
+            rows = wide(tile, 256)
+            part[rows, columns] = jnp.dot(
+                mixed_ref[rows, :], w_ref[:, columns], preferred_element_type=F32
+            ).astype(BF16)
+
+    for k in range(2):
+        project(x2, k)
+        go(part.at[top, chunk(x2, k)], relay_l.at[k], x_send.at[k], x_recv.at[k], right)
+        go(part.at[low, chunk(x2, k)], relay_r.at[k], x_send.at[2 + k], x_recv.at[2 + k], left)
+    for k in range(2):
+        project(x1, k)
+        go(part.at[low, chunk(x1, k)], direct_l.at[k, low], x_send.at[4 + k], x_recv.at[4 + k], right)
+        project(x3, k)
+        go(part.at[top, chunk(x3, k)], direct_r.at[k, top], x_send.at[6 + k], x_recv.at[6 + k], left)
+    for k in range(2):
+        project(x, k)
+
+    def weights(group):
+        @pl.loop(0, 2)
+        def _(tile):
+            rows = wide(tile, 256)
+            value = lax.dot_general(
+                mixed_ref[:, rows],
+                og_ref[:, pl.ds(512 * group, 512)],
+                (((0,), (0,)), ((), ())),
+                preferred_element_type=F32,
+            ).astype(BF16)
+            for j in range(4):
+                gw_part[j % 2, group // 2, (group % 2) * 2 + j // 2, rows, :] = value[:, 128 * j : 128 * j + 128]
+
+    for group in range(8):
+        weights(group)
+    go(gw_part.at[1 - c], gw_core, g_send.at[0], g_recv.at[0], core)
+
+    def relayed(k):
+        arrive(relay_l.at[k], x_recv.at[k])
+        part[top, chunk(x1, k)] = (part[top, chunk(x1, k)].astype(F32) + relay_l[k].astype(F32)).astype(BF16)
+        go(part.at[top, chunk(x1, k)], direct_l.at[k, top], x_send.at[8 + k], x_recv.at[8 + k], right)
+        arrive(relay_r.at[k], x_recv.at[2 + k])
+        part[low, chunk(x3, k)] = (part[low, chunk(x3, k)].astype(F32) + relay_r[k].astype(F32)).astype(BF16)
+        go(part.at[low, chunk(x3, k)], direct_r.at[k, low], x_send.at[10 + k], x_recv.at[10 + k], left)
+
+    relayed(0)
+    arrive(gw_core, g_recv.at[0])
+
+    for d in (1, 2, 3, 0):
+        yy = (y + d) % 4
+
+        @pl.loop(0, 4)
+        def _(z):
+            gw_sum[yy, z] = (gw_part[c, yy, z].astype(F32) + gw_core[yy, z].astype(F32)).astype(BF16)
+
+        if d:
+            go(gw_sum.at[yy], gw_ring.at[d - 1], g_send.at[d], g_recv.at[d], rings[d - 1])
+
+    relayed(1)
+
+    def combined(k):
+        arrive(direct_l.at[k, low], x_recv.at[4 + k])
+        arrive(direct_r.at[k, top], x_recv.at[6 + k])
+        arrive(direct_l.at[k, top], x_recv.at[8 + k])
+        arrive(direct_r.at[k, low], x_recv.at[10 + k])
+        return (
+            part[:, chunk(x, k)].astype(F32) + direct_l[k].astype(F32) + direct_r[k].astype(F32)
+        )
+
+    far_send[...] = combined(0).astype(BF16)
+    go(far_send, far_recv, z_send.at[0], z_recv.at[0], far)
+    for d in range(3):
+        arrive(gw_ring.at[d], g_recv.at[d + 1])
+
+    @pl.loop(0, 4)
+    def _(z):
+        gw_line[z] = (
+            gw_sum[y, z].astype(F32)
+            + gw_ring[0, z].astype(F32)
+            + gw_ring[1, z].astype(F32)
+            + gw_ring[2, z].astype(F32)
+        ).astype(BF16)
+
+    for d in range(3):
+        go(gw_line.at[(zl + d + 1) % 4], gw_last.at[d], g_send.at[4 + d], g_recv.at[4 + d], lines[d])
+    total[...] = combined(1)
+    for d in range(3):
+        arrive(gw_last.at[d], g_recv.at[4 + d])
+    gw_ref[...] = (
+        gw_line[zl].astype(F32) + gw_last[0].astype(F32) + gw_last[1].astype(F32) + gw_last[2].astype(F32)
+    ).astype(BF16)
+    arrive(far_recv, z_recv.at[0])
+    out_ref[...] = (total[...] + far_recv[...].astype(F32)).astype(BF16)
+    for copy in sends:
+        copy.wait_send()
+
+
+def reduce(mixed, w_full, og_full):
+    vmem = pl.BlockSpec(memory_space=pltpu.VMEM)
+    dma = pltpu.SemaphoreType.DMA
+    return pl.pallas_call(
+        reduce_kernel,
+        out_shape=(jax.ShapeDtypeStruct((768, 512), BF16), jax.ShapeDtypeStruct((512, 128), BF16)),
+        in_specs=[vmem] * 3,
+        out_specs=(vmem, vmem),
+        scratch_shapes=[
+            pltpu.VMEM((768, 4096), BF16),
+            pltpu.VMEM((2, 384, 512), BF16),
+            pltpu.VMEM((2, 384, 512), BF16),
+            pltpu.VMEM((2, 768, 512), BF16),
+            pltpu.VMEM((2, 768, 512), BF16),
+            pltpu.VMEM((768, 512), BF16),
+            pltpu.VMEM((768, 512), BF16),
+            pltpu.VMEM((768, 512), F32),
+            pltpu.VMEM((2, 4, 4, 512, 128), BF16),
+            pltpu.VMEM((4, 4, 512, 128), BF16),
+            pltpu.VMEM((4, 4, 512, 128), BF16),
+            pltpu.VMEM((3, 4, 512, 128), BF16),
+            pltpu.VMEM((4, 512, 128), BF16),
+            pltpu.VMEM((3, 512, 128), BF16),
+            dma((12,)),
+            dma((12,)),
+            dma((1,)),
+            dma((1,)),
+            dma((7,)),
+            dma((7,)),
+        ],
+        compiler_params=pltpu.CompilerParams(
+            collective_id=1, has_side_effects=True, vmem_limit_bytes=60 * 2**20
+        ),
+    )(mixed, w_full, og_full)
 
 
 def shifted(value, axis, steps):
@@ -51,13 +377,7 @@
     all_rows = local_rows * sequence_count
     column_width = ROW_LENGTH // sequence_count
     factor = HEAD_WIDTH ** (-0.5)
-    contract_last = (((1,), (1,)), ((), ()))
-    weight_rows = lax.all_gather(weight_out, "seq", axis=1, tiled=True)
-    grad_full = lax.all_gather(output_gradient, "mp", axis=1, tiled=True)
-    grad_wide = lax.dot_general(
-        grad_full, weight_rows, contract_last, preferred_element_type=jnp.float32
-    )
-    grad_mixed = grad_wide.astype(jnp.bfloat16)
+    weight_rows, grad_full, grad_mixed = gather(weight_out, output_gradient)
 
     def rows_of(input_tensor):
         return input_tensor[:, :half_width].reshape(local_rows, ROW_LENGTH, head_halves, HEAD_WIDTH)
@@ -152,19 +472,7 @@
     grad_query = join(row_gquery.astype(jnp.bfloat16), returned[1])
     grad_key = join(own_key.astype(jnp.bfloat16), returned[2])
     grad_value = join(own_value.astype(jnp.bfloat16), returned[3])
-    value_portion = jnp.dot(mixed, weight_rows, preferred_element_type=jnp.float32)
-    output = lax.psum_scatter(
-        value_portion.astype(jnp.bfloat16), "mp", scatter_dimension=1, tiled=True
-    )
-    summed = lax.psum_scatter(
-        lax.dot_general(
-            grad_full, mixed, (((0,), (0,)), ((), ())), preferred_element_type=jnp.float32
-        ).astype(jnp.bfloat16),
-        "seq",
-        scatter_dimension=0,
-        tiled=True,
-    ).astype(jnp.float32)
-    grad_weight = summed.T.astype(jnp.bfloat16)
+    output, grad_weight = reduce(mixed, weight_rows, grad_full)
     return (output, grad_query, grad_key, grad_value, grad_weight)
 
 

time: 684 us -> 318 us (0.46)
  waiting for transfers between devices: 552 us -> 27.9 us
  Pallas kernels: 0 us -> 199 us
  matrix products: 32.5 us -> 10.4 us
  between operations: 14.4 us -> 1.3 us
    all_gather x2 -> x0, waiting for transfers between devices: 212 us -> none  [the longest x1 142 us: per_device(): grad_full = lax.all_gather(output_gradient, 'mp', axis=1, tiled=True)]
    pallas_call x0 -> x2, Pallas kernels: none -> 199 us  [the longest x1 104 us: reduce(): pl.pallas_call(reduce_kernel, out_shape=(jax.ShapeDtypeStruct((768, 512),...]
    reduce_scatter x1 -> x0, waiting for transfers between devices: 168 us -> none  [per_device(): lax.psum_scatter(value_portion.astype(jnp.bfloat16), 'mp', scatter_dimens...]
    unnamed x5 -> x0, waiting for transfers between devices: 124 us -> none
    all_to_all x1, waiting for transfers between devices: 33.5 us -> 4.83 us  [per_device(): lax.all_to_all(packed, 'seq', split_axis=2, concat_axis=1, tiled=True)]
    dot_general x3 -> x0, matrix products: 22.8 us -> none  [the longest x1 7.87 us: per_device(): lax.dot_general(grad_full, mixed, (((0,), (0,)), ((), ())), preferred_ele...]
    unnamed x55 -> x57, local copies, waits for them, and re-layouts: 16.8 us -> 7.05 us
  transfers between devices with their start and end apart: 8 -> 4, of which waited for: 7 -> 4; matrix products, arithmetic and copies ran while one was open for 7% -> 12% of each run, Pallas kernels for 0% -> 0%
where the time goes in v1:
time: 318 us; the launch traced here: 314 us
  Pallas kernels  199 us (63%)
  local copies, waits for them, and re-layouts  38 us (12%)
  waiting for transfers between devices  27.9 us (9%)
  starting transfers between devices  26.6 us (8%)
  other arithmetic  11.4 us (4%)
  matrix products  10.4 us (3%)
    pallas_call x1, Pallas kernels, reduce(): pl.pallas_call(reduce_kernel, out_shape=(jax.ShapeDtypeStruct((768, 512),...  104 us
    pallas_call x1, Pallas kernels, gather(): pl.pallas_call(gather_kernel, out_shape=(jax.ShapeDtypeStruct((512, 4096)...  94.6 us
    ppermute x2, waiting for transfers between devices, shifted(): lax.ppermute(value, axis, [(source, source + steps) for source in range(i...  19.8 us
    all_to_all x1, starting transfers between devices, per_device(): lax.all_to_all(results, 'seq', split_axis=1, concat_axis=2, tiled=True)  14.5 us
    all_to_all x1, starting transfers between devices, per_device(): lax.all_to_all(packed, 'seq', split_axis=2, concat_axis=1, tiled=True)  7.9 us
    unnamed x57, local copies, waits for them, and re-layouts  7.05 us
  transfers between devices with their start and end apart: 4, of which 4 were waited for; matrix products, arithmetic and copies ran while one was open for 12% of the time, Pallas kernels for 0%

profile of v1, /device:TPU:96, one launch (start us, length us, event | category | flops | bytes accessed | tf_op | source)
XLA Modules:
  0.0 314.4 jit_solution(16632082466511907951)
XLA Ops:
  0.7 2.0 fusion.37
  2.7 0.8 fusion.36
  3.5 0.8 fusion.35
  4.3 94.6 %shard_map.92 = (bf16[512,4096]{1,0:T(8,128)(2,1)}, bf16[768,4096]{1,0:T(8,128)(2,1)}, bf16[768,512]{1,0:T(8,128)(2,1)}) custom-call(bf16[512,128]{1,0:T(8,128)(2,1)} %w_ref.1, bf16[768,512]{1,0:T(8,128)(2,1)} %og_ref.1), custom_call_target="tpu_custom_call" | custom-call | tf_op jit(solution)/shard_map/pallas_call | solution.py:154
  98.9 1.9 fusion.34
  101.0 2.3 copy.167
  103.3 7.9 %all-to-all-start = ((bf16[4,3,256,256]{3,0,1,2:T(4,128)(2,1)}), bf16[4,3,256,256]{3,0,1,2:T(4,128)(2,1)S(1)}, u32[]{:S(2)}, u32[]{:S(2)}) async-start(bf16[4,3,256,256]{3,0,1,2:T(4,128)(2,1)} %copy.167), calls=%async_computation | async-start | bytes 3145728 | tf_op jit(solution)/shard_map/all_to_all | solution.py:389
  111.5 0.7 pad_maximum_fusion.13
  112.2 2.0 collective-permute-start
  114.3 1.1 reshape.170
  115.5 0.7 fusion.19
  116.5 0.7 slice.139
  117.2 1.0 slice.134
  118.2 1.0 copy.187
  119.3 1.0 slice.140
  120.3 0.7 copy.162
  121.1 0.9 copy.159
  122.1 0.4 copy.186
  122.5 1.1 reshape.165
  123.6 0.8 copy.163
  124.5 1.0 copy.160
  125.6 1.2 copy.210
  127.0 10.0 %collective-permute-done = bf16[2,256,256]{1,2,0:T(8,128)(2,1)} collective-permute-done((bf16[2,256,256]{1,2,0:T(8,128)(2,1)}, bf16[2,256,256]{1,2,0:T(8,128)(2,1)}, u32[]{:S(2)}, u32[]{:S(2)}) %collective-permute-start) | collective-permute-done | bytes 262176 | tf_op jit(solution)/shard_map/ppermute | solution.py:339
  137.0 1.6 fusion.39
  138.8 0.6 fusion.22
  139.5 1.8 fusion.41
  141.5 4.8 %all-to-all-done = bf16[4,3,256,256]{3,0,1,2:T(4,128)(2,1)S(1)} async-done(((bf16[4,3,256,256]{3,0,1,2:T(4,128)(2,1)}), bf16[4,3,256,256]{3,0,1,2:T(4,128)(2,1)S(1)}, u32[]{:S(2)}, u32[]{:S(2)}) %all-to-all-start) | async-done | bytes 1572896 | tf_op jit(solution)/shard_map/all_to_all | solution.py:389
  147.1 1.9 fusion.40
  149.0 1.2 divide_convert_fusion.1
  150.5 0.6 fusion.18
  152.2 1.0 copy.229
  153.2 1.3 copy.175
  154.6 14.5 %all-to-all-start.1 = ((bf16[4,96,8,256]{3,2,0,1:T(8,128)(2,1)}), bf16[4,96,8,256]{3,2,0,1:T(8,128)(2,1)S(1)}, u32[]{:S(2)}, u32[]{:S(2)}) async-start(bf16[4,96,8,256]{3,2,0,1:T(8,128)(2,1)} %copy.175), calls=%async_computation.1 | async-start | bytes 3145728 | tf_op jit(solution)/shard_map/all_to_all | solution.py:462
  169.1 2.6 multiply_reduce_fusion
  171.8 0.7 multiply_convert_fusion
  172.5 0.6 multiply_bitcast_fusion
  173.1 0.5 copy-done.8
  173.6 0.7 slice.225
  174.3 0.8 slice.179
  175.2 0.6 convolution_bitcast_fusion
  175.8 0.7 slice.224
  176.5 0.5 copy-done.2
  177.0 0.8 slice.187
  177.8 1.3 copy.166
  179.1 0.8 copy.235
  179.9 1.5 fusion.17
  181.5 1.1 copy.183
  182.6 1.1 copy.234
  183.8 1.1 pad_maximum_fusion.14
  184.9 2.2 collective-permute-start.1
  187.5 0.7 slice.222
  188.2 9.8 %collective-permute-done.1 = bf16[2,256,256]{1,2,0:T(8,128)(2,1)S(1)} collective-permute-done((bf16[2,256,256]{1,2,0:T(8,128)(2,1)S(1)}, bf16[2,256,256]{1,2,0:T(8,128)(2,1)S(1)}, u32[]{:S(2)}, u32[]{:S(2)}) %collective-permute-start.1) | collective-permute-done | bytes 262176 | tf_op jit(solution)/shard_map/ppermute | solution.py:339
  198.0 0.7 fusion.38
  198.8 0.4 copy.189
  199.3 1.0 fusion.25
  200.4 0.4 copy.191
  200.9 3.3 %all-to-all-done.1 = bf16[4,96,8,256]{3,2,0,1:T(8,128)(2,1)S(1)} async-done(((bf16[4,96,8,256]{3,2,0,1:T(8,128)(2,1)}), bf16[4,96,8,256]{3,2,0,1:T(8,128)(2,1)S(1)}, u32[]{:S(2)}, u32[]{:S(2)}) %all-to-all-start.1) | async-done | bytes 1572896 | tf_op jit(solution)/shard_map/all_to_all | solution.py:462
  204.5 0.8 copy-done.13
  205.4 0.9 pad_maximum_fusion.3.mixed_ref
  206.3 104.2 %shard_map.93 = (bf16[768,512]{1,0:T(8,128)(2,1)}, bf16[512,128]{1,0:T(8,128)(2,1)}) custom-call(bf16[768,512]{1,0:T(8,128)(2,1)} %pad_maximum_fusion.3.mixed_ref, bf16[512,4096]{1,0:T(8,128)(2,1)} %get-tuple-element.11.w_ref, bf16[768,4096]{1,0:T(8,128)(2,1)} %get-tuple-element.12.og_ref), custom_call_target="tpu_custom_call" | custom-call | tf_op jit(solution)/shard_map/pallas_call | solution.py:303
  310.6 0.9 pad_maximum_fusion.6
  311.5 1.3 pad_maximum_fusion.4
  312.9 0.9 copy.238
  313.8 0.7 copy.239
  (84 shorter events, 4.9 us)
Async XLA Ops:
  0.6 2.1 copy-start.6
  0.6 2.8 copy-start.7
  103.3 43.0 %all-to-all-start = ((bf16[4,3,256,256]{3,0,1,2:T(4,128)(2,1)}), bf16[4,3,256,256]{3,0,1,2:T(4,128)(2,1)S(1)}, u32[]{:S(2)}, u32[]{:S(2)}) async-start(bf16[4,3,256,256]{3,0,1,2:T(4,128)(2,1)} %copy.167), calls=%async_computation | async-start | bytes 3145728 | tf_op jit(solution)/shard_map/all_to_all | solution.py:389
  112.2 24.8 %collective-permute-start = (bf16[2,256,256]{1,2,0:T(8,128)(2,1)}, bf16[2,256,256]{1,2,0:T(8,128)(2,1)}, u32[]{:S(2)}, u32[]{:S(2)}) collective-permute-start(bf16[2,256,256]{1,2,0:T(8,128)(2,1)} %pad_maximum_fusion.13), channel_id=1, source_target_pairs={{0,8},{8,16},{16,24},{24,32},{32,40},{40,48},{48,56},{56,64},{64,7... | collective-permute-start | bytes 786440 | tf_op jit(solution)/shard_map/ppermute | solution.py:339
  118.2 3.7 %copy-start.12 = (bf16[768,256]{1,0:T(8,128)(2,1)S(1)}, bf16[768,256]{1,0:T(8,128)(2,1)}, u32[]{:S(2)}) copy-start(bf16[768,256]{1,0:T(8,128)(2,1)} %get-tuple-element.25) | copy-start | bytes 1179652
  122.0 2.4 copy-start.11
  124.5 2.2 copy-start.19
  125.5 13.2 %copy-start.14 = (bf16[3,256,2,128]{3,1,2,0:T(8,128)(2,1)S(1)}, bf16[3,256,2,128]{3,1,2,0:T(8,128)(2,1)}, u32[]{:S(2)}) copy-start(bf16[3,256,2,128]{3,1,2,0:T(8,128)(2,1)} %copy.163) | copy-start | bytes 1179652
  125.5 13.3 %copy-start.16 = (bf16[2,256,2,128]{3,1,2,0:T(8,128)(2,1)S(1)}, bf16[2,256,2,128]{3,1,2,0:T(8,128)(2,1)}, u32[]{:S(2)}) copy-start(bf16[2,256,2,128]{3,1,2,0:T(8,128)(2,1)} %copy.162) | copy-start | bytes 786436
  138.8 0.7 copy-start.18
  154.6 49.6 %all-to-all-start.1 = ((bf16[4,96,8,256]{3,2,0,1:T(8,128)(2,1)}), bf16[4,96,8,256]{3,2,0,1:T(8,128)(2,1)S(1)}, u32[]{:S(2)}, u32[]{:S(2)}) async-start(bf16[4,96,8,256]{3,2,0,1:T(8,128)(2,1)} %copy.175), calls=%async_computation.1 | async-start | bytes 3145728 | tf_op jit(solution)/shard_map/all_to_all | solution.py:462
  169.1 2.7 copy-start.10
  169.1 2.7 copy-start.20
  169.1 2.7 copy-start.21
  169.1 2.7 copy-start.23
  172.5 1.1 copy-start.8
  173.6 2.2 copy-start
  175.8 1.2 copy-start.2
  175.8 4.1 %copy-start.9 = (bf16[3,2,256,512]{2,3,1,0:T(8,128)(2,1)S(1)}, bf16[3,2,256,512]{2,3,1,0:T(8,128)(2,1)}, u32[]{:S(2)}) copy-start(bf16[3,2,256,512]{2,3,1,0:T(8,128)(2,1)} %copy-done.8) | copy-start | bytes 4718596
  181.5 5.6 %copy-start.1 = (f32[3,512,2,128]{1,3,2,0:T(8,128)S(1)}, f32[3,512,2,128]{1,3,2,0:T(8,128)}, u32[]{:S(2)}) copy-start(f32[3,512,2,128]{1,3,2,0:T(8,128)} %copy-done) | copy-start | bytes 4718596
  182.6 4.5 %copy-start.4 = (f32[2,256,2,128]{1,3,2,0:T(8,128)S(1)}, f32[2,256,2,128]{1,3,2,0:T(8,128)}, u32[]{:S(2)}) copy-start(f32[2,256,2,128]{1,3,2,0:T(8,128)} %slice.179) | copy-start | bytes 1572868
  183.7 3.6 %copy-start.3 = (f32[3,512,2,128]{1,3,2,0:T(8,128)S(1)}, f32[3,512,2,128]{1,3,2,0:T(8,128)}, u32[]{:S(2)}) copy-start(f32[3,512,2,128]{1,3,2,0:T(8,128)} %copy-done.2) | copy-start | bytes 4718596
  183.7 3.6 %copy-start.5 = (f32[2,256,2,128]{1,3,2,0:T(8,128)S(1)}, f32[2,256,2,128]{1,3,2,0:T(8,128)}, u32[]{:S(2)}) copy-start(f32[2,256,2,128]{1,3,2,0:T(8,128)} %slice.187) | copy-start | bytes 1572868
  184.9 13.1 %collective-permute-start.1 = (bf16[2,256,256]{1,2,0:T(8,128)(2,1)S(1)}, bf16[2,256,256]{1,2,0:T(8,128)(2,1)S(1)}, u32[]{:S(2)}, u32[]{:S(2)}) collective-permute-start(bf16[2,256,256]{1,2,0:T(8,128)(2,1)S(1)} %bitcast.164), channel_id=1, source_target_pairs={{8,0},{16,8},{24,16},{32,24},{40,32},{48,40},{56,48},{64,56},{72,6... | collective-permute-start | bytes 786440 | tf_op jit(solution)/shard_map/ppermute | solution.py:339
  199.3 1.1 copy-start.15
  204.4 1.0 copy-start.13
  311.5 1.4 copy-start.17
  312.8 1.0 copy-start.22

commit v2 on v0

v2 whole, which is shorter than its diff:
```python
import jax
import jax.numpy as jnp
from jax import lax
from jax.experimental import pallas as pl
from jax.experimental.pallas import tpu as pltpu
from jax.sharding import PartitionSpec as P

HEAD_WIDTH = 128
ROW_LENGTH = 256
MESH = pl.DeviceIdType.MESH
F32 = jnp.float32
BF16 = jnp.bfloat16


def coords():
    s = lax.axis_index("seq")
    m = lax.axis_index("mp")
    return s // 8, (s // 2) % 4, s % 2, m // 2, m % 2


def device(y, zl, c, x, zh):
    return (y * 8 + zl * 2 + c, x * 2 + zh)


def remote(src, dst, send, recv, target):
    return pltpu.make_async_remote_copy(
        src_ref=src, dst_ref=dst, send_sem=send, recv_sem=recv, device_id=target, device_id_type=MESH
    )


def arrive(ref, sem):
    pltpu.make_async_copy(ref, ref, sem).wait()


def wide(index, width):
    return pl.ds(pl.multiple_of(index * width, width), width)


def dot(a, b, left, right):
    return lax.dot_general(a, b, (((left,), (right,)), ((), ())), preferred_element_type=F32)


def layer_kernel(
    q_ref, k_ref, v_ref, w_ref, og_ref,
    out_ref, gq_ref, gk_ref, gv_ref, gw_ref,
    w_buf, og_buf, row_q, row_k, row_v, row_p, gm, mixed, gk_sum, gv_sum, edge_out, edge_in,
    col_in, col_gm, col_out, col_f, col_p,
    part, relay_l, relay_r, direct_l, direct_r, far_send, far_recv, total,
    gw_part, gw_core, gw_sum, gw_ring, gw_line, gw_last,
    own_sem, w_send, w_recv, o_send, o_recv, b_send, b_recv, c_send, c_recv,
    x_send, x_recv, z_send, z_recv, g_send, g_recv,
):
    y, zl, c, x, zh = coords()
    s, m = lax.axis_index("seq"), lax.axis_index("mp")
    factor = HEAD_WIDTH ** (-0.5)
    core = device(y, zl, 1 - c, x, zh)
    lines = [device(y, (zl + d) % 4, c, x, zh) for d in (1, 2, 3)]
    rings = [device((y + d) % 4, zl, c, x, zh) for d in (1, 2, 3)]
    x1, x2, x3 = (x + 1) % 4, (x + 2) % 4, (x + 3) % 4
    right = device(y, zl, c, x1, zh)
    left = device(y, zl, c, x3, zh)
    far = device(y, zl, c, x, 1 - zh)
    after, before = ((s + 1) % 32, m), ((s + 31) % 32, m)

    barrier = pltpu.get_barrier_semaphore()
    for target in (right, left, far):
        pl.semaphore_signal(barrier, inc=1, device_id=target, device_id_type=MESH)

    @pl.loop(1, 32)
    def _(i):
        pl.semaphore_signal(barrier, inc=1, device_id=((s + i) % 32, m), device_id_type=MESH)

    pl.semaphore_wait(barrier, 34)

    sends = []

    def go(src, dst, send, recv, target):
        copy = remote(src, dst, send, recv, target)
        copy.start()
        sends.append(copy)

    def w_at(yy, zz, cc):
        return w_buf.at[:, wide(yy * 8 + zz * 2 + cc, 128)]

    def og_half(xx, hh, half):
        return og_buf.at[pl.ds(384 * half, 384), wide(xx * 2 + hh, 512)]

    def og_own(half):
        return og_ref.at[pl.ds(384 * half, 384)]

    local = []

    def keep(src, dst, sem):
        copy = pltpu.make_async_copy(src, dst, sem)
        copy.start()
        local.append(copy)

    for d in range(3):
        go(w_ref, w_at(y, zl, c), w_send.at[d], w_recv.at[d], lines[d])
    go(w_ref, w_at(y, zl, c), w_send.at[3], w_recv.at[3], core)
    go(og_own(0), og_half(x, zh, 0), o_send.at[0], o_recv.at[0], far)
    go(og_own(0), og_half(x, zh, 0), o_send.at[2], o_recv.at[2], right)
    go(og_own(1), og_half(x, zh, 1), o_send.at[4], o_recv.at[4], left)
    go(og_own(1), og_half(x, zh, 1), o_send.at[1], o_recv.at[1], far)
    go(og_own(1), og_half(x, zh, 1), o_send.at[3], o_recv.at[3], right)
    go(og_own(0), og_half(x, zh, 0), o_send.at[5], o_recv.at[5], left)
    row_part = pl.ds(0, 256)
    keep(q_ref.at[:, :, row_part], row_q, own_sem.at[0])
    keep(k_ref.at[:, :, row_part], row_k.at[pl.ds(1, 3)], own_sem.at[1])
    keep(v_ref.at[:, :, row_part], row_v.at[pl.ds(1, 3)], own_sem.at[2])
    keep(w_ref, w_at(y, zl, c), own_sem.at[3])
    keep(og_ref, og_buf.at[:, wide(m, 512)], own_sem.at[4])
    go(k_ref.at[2, :, row_part], row_k.at[0], b_send.at[0], b_recv.at[0], after)
    go(v_ref.at[2, :, row_part], row_v.at[0], b_send.at[1], b_recv.at[1], after)

    def spot(ref, owner):
        return ref.at[:, wide(owner // 2, 16), pl.ds(pl.multiple_of(256 + 128 * (owner % 2), 128), 128)]

    def to_columns(pairs, number):
        @pl.loop(1, 32)
        def _(i):
            peer = (s + i) % 32
            for src, dst in pairs:
                remote(
                    spot(src, peer), dst.at[pl.ds(3 * s, 3)], c_send.at[number], c_recv.at[number], (peer, m)
                ).start()

        for src, dst in pairs:
            pltpu.make_async_copy(spot(src, s), dst.at[pl.ds(3 * s, 3)], c_recv.at[number]).start()

    def to_rows(pairs, number):
        @pl.loop(1, 32)
        def _(i):
            peer = (s + i) % 32
            for n, (src, dst) in enumerate(pairs):
                remote(
                    src.at[pl.ds(3 * peer, 3)], spot(dst, s), c_send.at[number + n], c_recv.at[number + n], (peer, m)
                ).start()

        for n, (src, dst) in enumerate(pairs):
            pltpu.make_async_copy(src.at[pl.ds(3 * s, 3)], spot(dst, s), c_recv.at[number + n]).start()

    to_columns([(q_ref, col_in.at[0]), (k_ref, col_in.at[1]), (v_ref, col_in.at[2])], 0)

    seen = lax.broadcasted_iota(jnp.int32, (256, 256), 0) >= lax.broadcasted_iota(jnp.int32, (256, 256), 1)

    def head(h):
        return pl.ds(pl.multiple_of(128 * h, 128), 128)

    def row_forward(t, h):
        queries = row_q[t, :, head(h)]
        own = dot(queries, row_k[t + 1, :, head(h)], 1, 1)
        prior = dot(queries, row_k[t, :, head(h)], 1, 1)
        open_side = jnp.logical_or(t > 0, s > 0)
        prior = jnp.where(open_side, prior * factor, -1e30)
        scores = jnp.where(seen, own * factor, prior)
        weights = jnp.exp(scores - jnp.max(scores, axis=-1, keepdims=True))
        probs = (weights / jnp.sum(weights, axis=-1, keepdims=True)).astype(BF16)
        row_p[t, h] = probs
        zero = jnp.zeros_like(probs)
        outputs = dot(jnp.where(seen, probs, zero), row_v[t + 1, :, head(h)], 1, 0) + dot(
            jnp.where(seen, zero, probs), row_v[t, :, head(h)], 1, 0
        )
        mixed[t, :, head(h)] = outputs.astype(BF16)

    def row_backward(t, h):
        queries, probs, grads = row_q[t, :, head(h)], row_p[t, h], gm[t, :, head(h)]
        own = dot(grads, row_v[t + 1, :, head(h)], 1, 1)
        prior = dot(grads, row_v[t, :, head(h)], 1, 1)
        centre = jnp.sum(grads.astype(F32) * mixed[t, :, head(h)].astype(F32), axis=-1, keepdims=True)
        slopes = (probs.astype(F32) * (jnp.where(seen, own, prior) - centre)).astype(BF16)
        zero = jnp.zeros_like(probs)
        slopes_own, slopes_prior = jnp.where(seen, slopes, zero), jnp.where(seen, zero, slopes)
        probs_own, probs_prior = jnp.where(seen, probs, zero), jnp.where(seen, zero, probs)
        gq_ref[t, :, head(h)] = (
            (dot(slopes_own, row_k[t + 1, :, head(h)], 1, 0) + dot(slopes_prior, row_k[t, :, head(h)], 1, 0))
            * factor
        ).astype(BF16)
        gk_sum[t, :, head(h)] += dot(slopes_prior, queries, 0, 0)
        gv_sum[t, :, head(h)] += dot(probs_prior, grads, 0, 0)
        gk_sum[t + 1, :, head(h)] = dot(slopes_own, queries, 0, 0)
        gv_sum[t + 1, :, head(h)] = dot(probs_own, grads, 0, 0)

    below = lax.broadcasted_iota(jnp.int32, (96, 96), 0) >= lax.broadcasted_iota(jnp.int32, (96, 96), 1)

    def widen(src, dst):
        @pl.loop(0, 6)
        def _(i):
            dst[wide(i, 256), :] = src[wide(i, 16)].astype(F32).reshape(256, 128)

    def narrow(src, dst):
        @pl.loop(0, 6)
        def _(i):
            dst[wide(i, 16)] = src[wide(i, 256), :].astype(BF16).reshape(16, 16, 128)

    def column(j):
        return pl.ds(j, 96, stride=16)

    def col_forward(j):
        queries, keys, values = (col_f[a, column(j), :].astype(BF16) for a in range(3))
        scores = jnp.where(below, dot(queries, keys, 1, 1) * factor, -1e30)
        weights = jnp.exp(scores - jnp.max(scores, axis=-1, keepdims=True))
        probs = (weights / jnp.sum(weights, axis=-1, keepdims=True)).astype(BF16)
        col_p[j] = probs
        col_f[3, column(j), :] = dot(probs, values, 1, 0).astype(BF16).astype(F32)

    def col_backward(j):
        queries, keys, values = (col_f[a, column(j), :].astype(BF16) for a in range(3))
        outputs, wide_grads = col_f[3, column(j), :], col_f[4, column(j), :]
        probs, grads = col_p[j], wide_grads.astype(BF16)
        centre = jnp.sum(wide_grads * outputs, axis=-1, keepdims=True)
        slopes = (probs.astype(F32) * (dot(grads, values, 1, 1) - centre)).astype(BF16)
        col_f[0, column(j), :] = dot(slopes, keys, 1, 0) * factor
        col_f[1, column(j), :] = dot(slopes, queries, 0, 0) * factor
        col_f[2, column(j), :] = dot(probs, grads, 0, 0)

    def columns_of(body):
        @pl.loop(0, 4)
        def _(g):
            for b in range(4):
                body(4 * g + b)

    def add_gm(xx, hh, first=False):
        @pl.loop(0, 3)
        def _(t):
            value = dot(og_buf[wide(t, 256), wide(xx * 2 + hh, 512)], w_buf[:, wide(xx * 2 + hh, 512)], 1, 1)
            if first:
                total[t] = value
            else:
                total[t] += value

    halves = (1 - zh, zh)
    top, low = pl.ds(0, 384), pl.ds(384, 384)

    def chunk(xx, k):
        return wide(xx * 2 + halves[k], 512)

    def project(xx, k):
        columns = chunk(xx, k)

        @pl.loop(0, 3)
        def _(t):
            part[wide(t, 256), columns] = jnp.dot(
                mixed[t], w_buf[:, columns], preferred_element_type=F32
            ).astype(BF16)

    for copy in local[:3]:
        copy.wait()

    @pl.loop(2, 6)
    def _(u):
        row_forward(u // 2, u % 2)

    arrive(og_half(x3, zh, 0), o_recv.at[2])
    go(og_half(x3, zh, 0), og_half(x3, zh, 0), o_send.at[6], o_recv.at[6], right)
    arrive(og_half(x1, zh, 1), o_recv.at[4])
    go(og_half(x1, zh, 1), og_half(x1, zh, 1), o_send.at[7], o_recv.at[7], left)
    local[3].wait()
    number = 4
    for d in range(3):
        arrive(w_at(y, (zl + 3 - d) % 4, c), w_recv.at[d])
    for d in range(3):
        for k in range(4):
            block = w_at(y, (zl + k) % 4, c)
            go(block, block, w_send.at[number], w_recv.at[number], rings[d])
            number += 1
    for k in range(1, 4):
        block = w_at(y, (zl + k) % 4, c)
        go(block, block, w_send.at[number], w_recv.at[number], core)
        number += 1
    for b in range(2):
        arrive((row_k, row_v)[b].at[0], b_recv.at[b])

    @pl.loop(0, 2)
    def _(h):
        row_forward(0, h)

    for half in range(2):
        block = og_half(x, 1 - zh, half)
        arrive(block, o_recv.at[half])
        go(block, block, o_send.at[8 + half], o_recv.at[8 + half], right)
        go(block, block, o_send.at[10 + half], o_recv.at[10 + half], left)
    arrive(col_in, c_recv.at[0])
    for a in range(3):
        widen(col_in.at[a], col_f.at[a])
    columns_of(col_forward)
    narrow(col_f.at[3], col_out.at[0])
    to_rows([(col_out.at[0], mixed)], 1)
    for d in range(3):
        for k in range(4):
            block = w_at((y + 3 - d) % 4, (zl + k) % 4, c)
            arrive(block, w_recv.at[4 + 4 * d + k])
            go(block, block, w_send.at[number], w_recv.at[number], core)
            number += 1
    arrive(og_half(x3, 1 - zh, 0), o_recv.at[8])
    go(og_half(x3, 1 - zh, 0), og_half(x3, 1 - zh, 0), o_send.at[12], o_recv.at[12], right)
    arrive(og_half(x1, 1 - zh, 1), o_recv.at[11])
    go(og_half(x1, 1 - zh, 1), og_half(x1, 1 - zh, 1), o_send.at[13], o_recv.at[13], left)
    arrive(w_at(y, zl, 1 - c), w_recv.at[3])
    for k in range(1, 4):
        arrive(w_at(y, (zl + k) % 4, 1 - c), w_recv.at[15 + k])
    for d in range(3):
        for k in range(4):
            arrive(w_at((y + 3 - d) % 4, (zl + k) % 4, 1 - c), w_recv.at[19 + 4 * d + k])
    local[4].wait()
    add_gm(x, zh, True)
    arrive(og_half(x3, zh, 1), o_recv.at[3])
    add_gm(x3, zh)
    arrive(og_half(x1, zh, 0), o_recv.at[5])
    add_gm(x1, zh)
    arrive(og_half(x2, zh, 0), o_recv.at[6])
    arrive(og_half(x2, zh, 1), o_recv.at[7])
    add_gm(x2, zh)
    add_gm(x, 1 - zh)

    arrive(mixed.at[:, :, pl.ds(256, 256)], c_recv.at[1])
    for k in range(2):
        project(x2, k)
        go(part.at[top, chunk(x2, k)], relay_l.at[k], x_send.at[k], x_recv.at[k], right)
        go(part.at[low, chunk(x2, k)], relay_r.at[k], x_send.at[2 + k], x_recv.at[2 + k], left)
    arrive(og_half(x3, 1 - zh, 1), o_recv.at[9])
    add_gm(x3, 1 - zh)
    arrive(og_half(x1, 1 - zh, 0), o_recv.at[10])
    add_gm(x1, 1 - zh)
    arrive(og_half(x2, 1 - zh, 0), o_recv.at[12])
    arrive(og_half(x2, 1 - zh, 1), o_recv.at[13])
    add_gm(x2, 1 - zh)

    @pl.loop(0, 3)
    def _(t):
        gm[t] = total[t].astype(BF16)

    to_columns([(gm, col_gm)], 2)
    for k in range(2):
        project(x1, k)
        go(part.at[low, chunk(x1, k)], direct_l.at[k, low], x_send.at[4 + k], x_recv.at[4 + k], right)
        project(x3, k)
        go(part.at[top, chunk(x3, k)], direct_r.at[k, top], x_send.at[6 + k], x_recv.at[6 + k], left)

    def relayed(k):
        arrive(relay_l.at[k], x_recv.at[k])
        part[top, chunk(x1, k)] = (part[top, chunk(x1, k)].astype(F32) + relay_l[k].astype(F32)).astype(BF16)
        go(part.at[top, chunk(x1, k)], direct_l.at[k, top], x_send.at[8 + k], x_recv.at[8 + k], right)
        arrive(relay_r.at[k], x_recv.at[2 + k])
        part[low, chunk(x3, k)] = (part[low, chunk(x3, k)].astype(F32) + relay_r[k].astype(F32)).astype(BF16)
        go(part.at[low, chunk(x3, k)], direct_r.at[k, low], x_send.at[10 + k], x_recv.at[10 + k], left)

    relayed(0)
    gk_sum[0] = jnp.zeros_like(gk_sum[0])
    gv_sum[0] = jnp.zeros_like(gv_sum[0])

    @pl.loop(0, 2)
    def _(h):
        row_backward(0, h)

    edge_out[0] = (gk_sum[0] * factor).astype(BF16)
    edge_out[1] = gv_sum[0].astype(BF16)
    go(edge_out, edge_in, b_send.at[2], b_recv.at[2], before)
    arrive(col_gm, c_recv.at[2])
    widen(col_gm, col_f.at[4])
    columns_of(col_backward)
    for a in range(3):
        narrow(col_f.at[a], col_out.at[a + 1])
    to_rows([(col_out.at[1], gq_ref), (col_out.at[2], gk_ref), (col_out.at[3], gv_ref)], 3)
    relayed(1)
    for k in range(2):
        project(x, k)

    for group in range(8):

        @pl.loop(0, 2)
        def _(tile):
            rows = wide(tile, 256)
            value = jnp.zeros((256, 512), F32)
            for t in range(3):
                value += dot(mixed[t, :, rows], og_buf[pl.ds(256 * t, 256), pl.ds(512 * group, 512)], 0, 0)
            value = value.astype(BF16)
            for j in range(4):
                gw_part[j % 2, group // 2, (group % 2) * 2 + j // 2, rows, :] = value[:, 128 * j : 128 * j + 128]

    go(gw_part.at[1 - c], gw_core, g_send.at[0], g_recv.at[0], core)

    def combined(k, t):
        rows = wide(t, 256)
        return (
            part[rows, chunk(x, k)].astype(F32) + direct_l[k, rows].astype(F32) + direct_r[k, rows].astype(F32)
        )

    def ready(k):
        arrive(direct_l.at[k, low], x_recv.at[4 + k])
        arrive(direct_r.at[k, top], x_recv.at[6 + k])
        arrive(direct_l.at[k, top], x_recv.at[8 + k])
        arrive(direct_r.at[k, low], x_recv.at[10 + k])

    ready(0)

    @pl.loop(0, 3)
    def _(t):
        far_send[t] = combined(0, t).astype(BF16)

    go(far_send, far_recv, z_send.at[0], z_recv.at[0], far)
    arrive(gw_core, g_recv.at[0])

    for d in (1, 2, 3, 0):
        yy = (y + d) % 4

        @pl.loop(0, 4)
        def _(z):
            gw_sum[yy, z] = (gw_part[c, yy, z].astype(F32) + gw_core[yy, z].astype(F32)).astype(BF16)

        if d:
            go(gw_sum.at[yy], gw_ring.at[d - 1], g_send.at[d], g_recv.at[d], rings[d - 1])

    @pl.loop(2, 6)
    def _(u):
        row_backward(u // 2, u % 2)

    ready(1)

    @pl.loop(0, 3)
    def _(t):
        total[t] = combined(1, t)

    for d in range(3):
        arrive(gw_ring.at[d], g_recv.at[d + 1])

    @pl.loop(0, 4)
    def _(z):
        gw_line[z] = (
            gw_sum[y, z].astype(F32)
            + gw_ring[0, z].astype(F32)
            + gw_ring[1, z].astype(F32)
            + gw_ring[2, z].astype(F32)
        ).astype(BF16)

    for d in range(3):
        go(gw_line.at[(zl + d + 1) % 4], gw_last.at[d], g_send.at[4 + d], g_recv.at[4 + d], lines[d])

    arrive(edge_in, b_recv.at[2])

    @pl.loop(0, 3)
    def _(t):
        edge_k = jnp.where(t == 2, edge_in[0].astype(F32), 0.0)
        edge_v = jnp.where(t == 2, edge_in[1].astype(F32), 0.0)
        gk_ref[t, :, row_part] = (gk_sum[t + 1] * factor + edge_k).astype(BF16)
        gv_ref[t, :, row_part] = (gv_sum[t + 1] + edge_v).astype(BF16)

    for d in range(3):
        arrive(gw_last.at[d], g_recv.at[4 + d])
    gw_ref[...] = (
        gw_line[zl].astype(F32) + gw_last[0].astype(F32) + gw_last[1].astype(F32) + gw_last[2].astype(F32)
    ).astype(BF16)
    arrive(far_recv, z_recv.at[0])

    @pl.loop(0, 3)
    def _(t):
        out_ref[t] = (total[t] + far_recv[t].astype(F32)).astype(BF16)

    for n, ref in enumerate((gq_ref, gk_ref, gv_ref)):
        arrive(ref.at[:, :, pl.ds(256, 256)], c_recv.at[3 + n])
    arrive(col_in.at[:, pl.ds(0, 93)], c_send.at[0])
    arrive(col_out.at[0, pl.ds(0, 93)], c_send.at[1])
    arrive(col_gm.at[pl.ds(0, 93)], c_send.at[2])
    for n in range(3):
        arrive(col_out.at[n + 1, pl.ds(0, 93)], c_send.at[3 + n])
    for copy in sends:
        copy.wait_send()


def per_device(query, key, value, weight_out, output_gradient):
    rows = jax.ShapeDtypeStruct((3, 256, 512), BF16)
    any_space = pl.BlockSpec(memory_space=pl.ANY)
    vmem = pl.BlockSpec(memory_space=pltpu.VMEM)
    dma = pltpu.SemaphoreType.DMA

    def half(*shape):
        return pltpu.VMEM(shape, BF16)

    def full(*shape):
        return pltpu.VMEM(shape, F32)

    output, grad_query, grad_key, grad_value, grad_weight = pl.pallas_call(
        layer_kernel,
        out_shape=(rows, rows, rows, rows, jax.ShapeDtypeStruct((512, 128), BF16)),
        in_specs=[any_space] * 5,
        out_specs=(vmem,) * 5,
        scratch_shapes=[
            half(512, 4096),
            half(768, 4096),
            half(3, 256, 256),
            half(4, 256, 256),
            half(4, 256, 256),
            half(3, 2, 256, 256),
            half(3, 256, 512),
            half(3, 256, 512),
            full(4, 256, 256),
            full(4, 256, 256),
            half(2, 256, 256),
            half(2, 256, 256),
            half(3, 96, 16, 128),
            half(96, 16, 128),
            half(4, 96, 16, 128),
            full(5, 1536, 128),
            half(16, 96, 96),
            half(768, 4096),
            half(2, 384, 512),
            half(2, 384, 512),
            half(2, 768, 512),
            half(2, 768, 512),
            half(3, 256, 512),
            half(3, 256, 512),
            full(3, 256, 512),
            half(2, 4, 4, 512, 128),
            half(4, 4, 512, 128),
            half(4, 4, 512, 128),
            half(3, 4, 512, 128),
            half(4, 512, 128),
            half(3, 512, 128),
            dma((5,)),
            dma((31,)),
            dma((31,)),
            dma((14,)),
            dma((14,)),
            dma((3,)),
            dma((3,)),
            dma((6,)),
            dma((6,)),
            dma((12,)),
            dma((12,)),
            dma((1,)),
            dma((1,)),
            dma((7,)),
            dma((7,)),
        ],
        compiler_params=pltpu.CompilerParams(
            collective_id=0, has_side_effects=True, vmem_limit_bytes=62 * 2**20
        ),
    )(
        query.reshape(3, 256, 512),
        key.reshape(3, 256, 512),
        value.reshape(3, 256, 512),
        weight_out,
        output_gradient,
    )
    return (
        output.reshape(768, 512),
        grad_query.reshape(768, 512),
        grad_key.reshape(768, 512),
        grad_value.reshape(768, 512),
        grad_weight,
    )


def solution(mesh):
    in_specs = (P("seq", "mp"), P("seq", "mp"), P("seq", "mp"), P("mp", "seq"), P("seq", "mp"))
    out_specs = (P("seq", "mp"), P("seq", "mp"), P("seq", "mp"), P("seq", "mp"), P("mp", "seq"))
    return jax.shard_map(
        per_device, mesh=mesh, in_specs=in_specs, out_specs=out_specs, check_vma=False
    )
```

time: 684 us -> 208 us (0.30)
  waiting for transfers between devices: 552 us -> 0 us
  Pallas kernels: 0 us -> 198 us
  local copies, waits for them, and re-layouts: 44.3 us -> 6.65 us
  matrix products: 32.5 us -> 0 us
  starting transfers between devices: 24.8 us -> 0 us
  between operations: 14.4 us -> 0.65 us
  other arithmetic: 11 us -> 0 us
    all_gather x2 -> x0, waiting for transfers between devices: 212 us -> none  [the longest x1 142 us: per_device(): grad_full = lax.all_gather(output_gradient, 'mp', axis=1, tiled=True)]
    pallas_call x0 -> x1, Pallas kernels: none -> 198 us  [per_device(): pl.pallas_call(layer_kernel, out_shape=(rows, rows, rows, rows, jax.Shape...]
    reduce_scatter x1 -> x0, waiting for transfers between devices: 168 us -> none  [per_device(): lax.psum_scatter(value_portion.astype(jnp.bfloat16), 'mp', scatter_dimens...]
    unnamed x5 -> x0, waiting for transfers between devices: 124 us -> none
    all_to_all x2 -> x0, waiting for transfers between devices: 33.5 us -> none  [the longest x1 33.5 us: per_device(): lax.all_to_all(packed, 'seq', split_axis=2, concat_axis=1, tiled=True)]
    dot_general x14 -> x0, matrix products: 31.2 us -> none  [the longest x1 7.87 us: per_device(): lax.dot_general(grad_full, mixed, (((0,), (0,)), ((), ())), preferred_ele...]
    all_to_all x2 -> x0, starting transfers between devices: 20.5 us -> none  [the longest x1 12.4 us: per_device(): lax.all_to_all(packed, 'seq', split_axis=2, concat_axis=1, tiled=True)]
    ppermute x2 -> x0, waiting for transfers between devices: 14.8 us -> none  [shifted(): lax.ppermute(value, axis, [(source, source + steps) for source in range(i...]
  transfers between devices with their start and end apart: 8 -> 0, of which waited for: 7 -> 0; matrix products, arithmetic and copies ran while one was open for 7% -> 0% of each run, Pallas kernels for 0% -> 0%
where the time goes in v2:
time: 208 us; the launch traced here: 206 us
  Pallas kernels  198 us (95%)
  local copies, waits for them, and re-layouts  6.65 us (3%)
    pallas_call x1, Pallas kernels, per_device(): pl.pallas_call(layer_kernel, out_shape=(rows, rows, rows, rows, jax.Shape...  198 us
    unnamed x13, local copies, waits for them, and re-layouts  6.65 us

profile of v2, /device:TPU:96, one launch (start us, length us, event | category | flops | bytes accessed | tf_op | source)
XLA Modules:
  0.0 205.6 jit_solution(7430058251391917120)
XLA Ops:
  0.6 198.3 %shard_map.92 = (bf16[3,256,512]{2,1,0:T(8,128)(2,1)}, bf16[3,256,512]{2,1,0:T(8,128)(2,1)}, bf16[3,256,512]{2,1,0:T(8,128)(2,1)}, bf16[3,256,512]{2,1,0:T(8,128)(2,1)}, bf16[512,128]{1,0:T(8,128)(2,1)}) custom-call(bf16[3,256,512]{2,1,0:T(8,128)(2,1)} %bitcast.11, bf16[3,256,512]{2,1,0:T(8,128)(2,1)} %bitcast.12, bf16[3,256,512]{2,1,0:T(8,128)(2,1)} %bitcast.13, ...), custom_call_target="tpu_custom_call" | custom-call | tf_op jit(solution)/shard_map/pallas_call | solution.py:482
  198.9 0.0 copy-start.2
  198.9 2.1 %copy.15 = bf16[768,512]{1,0:T(8,128)(2,1)} copy(bf16[768,512]{1,0:T(8,128)(2,1)} %bitcast.10) | data formatting | bytes 1572864
  201.0 0.0 copy-done.2
  201.1 0.0 copy-start.1
  201.1 0.9 copy.16
  201.9 0.5 copy-done.1
  202.5 0.0 copy-start
  202.5 0.9 copy.17
  203.3 0.5 copy-done
  203.9 0.0 copy-start.3
  203.9 0.9 copy.18
  204.8 0.1 copy-done.3
  204.9 0.7 copy.19
Async XLA Ops:
  198.9 2.1 %copy-start.2 = (bf16[3,256,512]{2,1,0:T(8,128)(2,1)S(1)}, bf16[3,256,512]{2,1,0:T(8,128)(2,1)}, u32[]{:S(2)}) copy-start(bf16[3,256,512]{2,1,0:T(8,128)(2,1)} %get-tuple-element.11) | copy-start | bytes 2359300
  201.1 1.4 copy-start.1
  202.5 1.4 copy-start
  203.9 1.0 copy-start.3

commit v3 on v2

v3 whole, which is shorter than its diff:
```python
import jax
import jax.numpy as jnp
from jax import lax
from jax.experimental import pallas as pl
from jax.experimental.pallas import tpu as pltpu
from jax.sharding import PartitionSpec as P

HEAD_WIDTH = 128
ROW_LENGTH = 256
MESH = pl.DeviceIdType.MESH
F32 = jnp.float32
BF16 = jnp.bfloat16


def coords():
    s = lax.axis_index("seq")
    m = lax.axis_index("mp")
    return s // 8, (s // 2) % 4, s % 2, m // 2, m % 2


def device(y, zl, c, x, zh):
    return (y * 8 + zl * 2 + c, x * 2 + zh)


def remote(src, dst, send, recv, target):
    return pltpu.make_async_remote_copy(
        src_ref=src, dst_ref=dst, send_sem=send, recv_sem=recv, device_id=target, device_id_type=MESH
    )


def arrive(ref, sem):
    pltpu.make_async_copy(ref, ref, sem).wait()


def wide(index, width):
    return pl.ds(pl.multiple_of(index * width, width), width)


def dot(a, b, left, right):
    return lax.dot_general(a, b, (((left,), (right,)), ((), ())), preferred_element_type=F32)


def layer_kernel(
    q_ref, k_ref, v_ref, w_ref, og_ref,
    out_ref, gq_ref, gk_ref, gv_ref, gw_ref,
    w_buf, og_buf, row_q, row_k, row_v, row_p, gm_own, gm_far, gm_row, gm_in, mixed, mixed_far,
    gk_sum, gv_sum, edge_out, edge_in,
    col_in, col_gm, col_out, col_f, col_p,
    part, relay_l, relay_r, direct_l, direct_r, total,
    gw_part, gw_core, gw_sum, gw_ring, gw_line, gw_last,
    own_sem, w_send, w_recv, o_send, o_recv, b_send, b_recv, c_send, c_recv,
    x_send, x_recv, z_send, z_recv, g_send, g_recv,
):
    y, zl, c, x, zh = coords()
    s, m = lax.axis_index("seq"), lax.axis_index("mp")
    m_far = x * 2 + 1 - zh
    factor = HEAD_WIDTH ** (-0.5)
    core = device(y, zl, 1 - c, x, zh)
    rings = [device((y + d) % 4, zl, c, x, zh) for d in (1, 2, 3)]
    x1, x2, x3 = (x + 1) % 4, (x + 2) % 4, (x + 3) % 4
    right = device(y, zl, c, x1, zh)
    left = device(y, zl, c, x3, zh)
    far = device(y, zl, c, x, 1 - zh)
    after, before = ((s + 1) % 32, m), ((s + 31) % 32, m)
    user = zl // 2
    at_home = user == zh
    away = jnp.logical_not(at_home)

    barrier = pltpu.get_barrier_semaphore()
    for target in (right, left, far):
        pl.semaphore_signal(barrier, inc=1, device_id=target, device_id_type=MESH)

    @pl.loop(1, 32)
    def _(i):
        peer = (s + i) % 32
        pl.semaphore_signal(barrier, inc=1, device_id=(peer, m), device_id_type=MESH)
        pl.semaphore_signal(barrier, inc=1, device_id=(peer, m_far), device_id_type=MESH)

    pl.semaphore_wait(barrier, 65)

    sends = []

    def go(src, dst, send, recv, target):
        copy = remote(src, dst, send, recv, target)
        copy.start()
        sends.append(copy)

    def slot(yy, b, cc):
        return wide(yy * 4 + b * 2 + cc, 128)

    def og_half(xx, half):
        return og_buf.at[pl.ds(384 * half, 384), wide(xx, 512)]

    def og_own(half):
        return og_ref.at[pl.ds(384 * half, 384)]

    local = []

    def keep(src, dst, sem):
        copy = pltpu.make_async_copy(src, dst, sem)
        copy.start()
        local.append(copy)

    side = jnp.where(at_home, 0, 1)
    w_here = w_buf.at[side, :, slot(y, zl % 2, c)]
    w_index = side * 2 + zl % 2
    for d in range(1, 4):
        go(w_ref, w_here, w_send.at[d], w_recv.at[w_index], device(y, (zl + d) % 4, c, x, user))
    w_away = remote(w_ref, w_here, w_send.at[0], w_recv.at[w_index], far)
    w_home = pltpu.make_async_copy(w_ref, w_here, w_recv.at[w_index])

    @pl.when(away)
    def _():
        w_away.start()

    @pl.when(at_home)
    def _():
        w_home.start()

    go(og_own(0), og_half(x, 0), o_send.at[0], o_recv.at[0], right)
    go(og_own(1), og_half(x, 1), o_send.at[1], o_recv.at[1], left)
    go(og_own(1), og_half(x, 1), o_send.at[2], o_recv.at[2], right)
    go(og_own(0), og_half(x, 0), o_send.at[3], o_recv.at[3], left)
    row_part, col_part = pl.ds(0, 256), pl.ds(256, 256)
    keep(q_ref.at[:, :, row_part], row_q, own_sem.at[0])
    keep(k_ref.at[:, :, row_part], row_k.at[pl.ds(1, 3)], own_sem.at[1])
    keep(v_ref.at[:, :, row_part], row_v.at[pl.ds(1, 3)], own_sem.at[2])
    keep(og_ref, og_buf.at[:, wide(x, 512)], own_sem.at[3])
    go(k_ref.at[2, :, row_part], row_k.at[0], b_send.at[0], b_recv.at[0], after)
    go(v_ref.at[2, :, row_part], row_v.at[0], b_send.at[1], b_recv.at[1], after)

    def spot(ref, owner):
        return ref.at[:, wide(owner // 2, 16), pl.ds(pl.multiple_of(256 + 128 * (owner % 2), 128), 128)]

    def to_columns(pairs, number):
        @pl.loop(1, 32)
        def _(i):
            peer = (s + i) % 32
            for src, dst in pairs:
                remote(
                    spot(src, peer), dst.at[pl.ds(3 * s, 3)], c_send.at[number], c_recv.at[number], (peer, m)
                ).start()

        for src, dst in pairs:
            pltpu.make_async_copy(spot(src, s), dst.at[pl.ds(3 * s, 3)], c_recv.at[number]).start()

    def to_far_columns(src, dst, number):
        @pl.loop(0, 32)
        def _(i):
            peer = (s + i) % 32
            remote(
                spot(src, peer), dst.at[pl.ds(3 * s, 3)], c_send.at[number], c_recv.at[number], (peer, m_far)
            ).start()

    def to_rows(pairs, number):
        @pl.loop(1, 32)
        def _(i):
            peer = (s + i) % 32
            for n, (src, dst) in enumerate(pairs):
                remote(
                    src.at[pl.ds(3 * peer, 3)], spot(dst, s), c_send.at[number + n], c_recv.at[number + n], (peer, m)
                ).start()

        for n, (src, dst) in enumerate(pairs):
            pltpu.make_async_copy(src.at[pl.ds(3 * s, 3)], spot(dst, s), c_recv.at[number + n]).start()

    def to_far_rows(src, dst, number):
        @pl.loop(0, 32)
        def _(i):
            peer = (s + i) % 32
            remote(
                src.at[pl.ds(3 * peer, 3)], spot(dst, s), c_send.at[number], c_recv.at[number], (peer, m_far)
            ).start()

    to_columns([(q_ref, col_in.at[0]), (k_ref, col_in.at[1]), (v_ref, col_in.at[2])], 0)

    seen = lax.broadcasted_iota(jnp.int32, (256, 256), 0) >= lax.broadcasted_iota(jnp.int32, (256, 256), 1)

    def head(h):
        return pl.ds(pl.multiple_of(128 * h, 128), 128)

    def row_forward(t, h):
        queries = row_q[t, :, head(h)]
        own = dot(queries, row_k[t + 1, :, head(h)], 1, 1)
        prior = dot(queries, row_k[t, :, head(h)], 1, 1)
        open_side = jnp.logical_or(t > 0, s > 0)
        prior = jnp.where(open_side, prior * factor, -1e30)
        scores = jnp.where(seen, own * factor, prior)
        weights = jnp.exp(scores - jnp.max(scores, axis=-1, keepdims=True))
        probs = (weights / jnp.sum(weights, axis=-1, keepdims=True)).astype(BF16)
        row_p[t, h] = probs
        zero = jnp.zeros_like(probs)
        outputs = dot(jnp.where(seen, probs, zero), row_v[t + 1, :, head(h)], 1, 0) + dot(
            jnp.where(seen, zero, probs), row_v[t, :, head(h)], 1, 0
        )
        mixed[t, :, head(h)] = outputs.astype(BF16)

    def row_backward(t, h):
        queries, probs, grads = row_q[t, :, head(h)], row_p[t, h], gm_row[t, :, head(h)]
        own = dot(grads, row_v[t + 1, :, head(h)], 1, 1)
        prior = dot(grads, row_v[t, :, head(h)], 1, 1)
        centre = jnp.sum(grads.astype(F32) * mixed[t, :, head(h)].astype(F32), axis=-1, keepdims=True)
        slopes = (probs.astype(F32) * (jnp.where(seen, own, prior) - centre)).astype(BF16)
        zero = jnp.zeros_like(probs)
        slopes_own, slopes_prior = jnp.where(seen, slopes, zero), jnp.where(seen, zero, slopes)
        probs_own, probs_prior = jnp.where(seen, probs, zero), jnp.where(seen, zero, probs)
        gq_ref[t, :, head(h)] = (
            (dot(slopes_own, row_k[t + 1, :, head(h)], 1, 0) + dot(slopes_prior, row_k[t, :, head(h)], 1, 0))
            * factor
        ).astype(BF16)
        gk_sum[t, :, head(h)] += dot(slopes_prior, queries, 0, 0)
        gv_sum[t, :, head(h)] += dot(probs_prior, grads, 0, 0)
        gk_sum[t + 1, :, head(h)] = dot(slopes_own, queries, 0, 0)
        gv_sum[t + 1, :, head(h)] = dot(probs_own, grads, 0, 0)

    below = lax.broadcasted_iota(jnp.int32, (96, 96), 0) >= lax.broadcasted_iota(jnp.int32, (96, 96), 1)

    def widen(src, dst):
        @pl.loop(0, 6)
        def _(i):
            dst[wide(i, 256), :] = src[wide(i, 16)].astype(F32).reshape(256, 128)

    def narrow(src, dst):
        @pl.loop(0, 6)
        def _(i):
            dst[wide(i, 16)] = src[wide(i, 256), :].astype(BF16).reshape(16, 16, 128)

    def column(j):
        return pl.ds(j, 96, stride=16)

    def col_forward(j):
        queries, keys, values = (col_f[a, column(j), :].astype(BF16) for a in range(3))
        scores = jnp.where(below, dot(queries, keys, 1, 1) * factor, -1e30)
        weights = jnp.exp(scores - jnp.max(scores, axis=-1, keepdims=True))
        probs = (weights / jnp.sum(weights, axis=-1, keepdims=True)).astype(BF16)
        col_p[j] = probs
        col_f[3, column(j), :] = dot(probs, values, 1, 0).astype(BF16).astype(F32)

    def col_backward(j):
        queries, keys, values = (col_f[a, column(j), :].astype(BF16) for a in range(3))
        outputs, wide_grads = col_f[3, column(j), :], col_f[4, column(j), :]
        probs, grads = col_p[j], wide_grads.astype(BF16)
        centre = jnp.sum(wide_grads * outputs, axis=-1, keepdims=True)
        slopes = (probs.astype(F32) * (dot(grads, values, 1, 1) - centre)).astype(BF16)
        col_f[0, column(j), :] = dot(slopes, keys, 1, 0) * factor
        col_f[1, column(j), :] = dot(slopes, queries, 0, 0) * factor
        col_f[2, column(j), :] = dot(probs, grads, 0, 0)

    def columns_of(body):
        @pl.loop(0, 4)
        def _(g):
            for b in range(4):
                body(4 * g + b)

    top, low = pl.ds(0, 384), pl.ds(384, 384)

    def project(xx):
        columns = wide(xx, 512)

        @pl.loop(0, 3)
        def _(t):
            part[wide(t, 256), columns] = (
                dot(mixed[t], w_buf[0, :, columns], 1, 0) + dot(mixed_far[t], w_buf[1, :, columns], 1, 0)
            ).astype(BF16)

    for copy in local[:3]:
        copy.wait()

    @pl.loop(2, 6)
    def _(u):
        row_forward(u // 2, u % 2)

    arrive(og_half(x3, 0), o_recv.at[0])
    go(og_half(x3, 0), og_half(x3, 0), o_send.at[4], o_recv.at[4], right)
    arrive(og_half(x1, 1), o_recv.at[1])
    go(og_half(x1, 1), og_half(x1, 1), o_send.at[5], o_recv.at[5], left)
    for a in range(2):
        for b in range(2):
            arrive(w_buf.at[a, :, slot(y, b, c)], w_recv.at[2 * a + b])
    for d in range(3):
        for b in range(2):
            block = w_buf.at[:, :, slot(y, b, c)]
            go(block, block, w_send.at[4 + 2 * d + b], w_recv.at[4 + 2 * d + b], rings[d])
    for b in range(2):
        block = w_buf.at[:, :, slot(y, b, c)]
        go(block, block, w_send.at[10 + b], w_recv.at[10 + b], core)
    for b in range(2):
        arrive((row_k, row_v)[b].at[0], b_recv.at[b])

    @pl.loop(0, 2)
    def _(h):
        row_forward(0, h)

    arrive(col_in, c_recv.at[0])
    go(mixed.at[:, :, row_part], mixed_far.at[:, :, row_part], z_send.at[0], z_recv.at[0], far)
    for a in range(3):
        widen(col_in.at[a], col_f.at[a])
    columns_of(col_forward)
    narrow(col_f.at[3], col_out.at[0])
    to_rows([(col_out.at[0], mixed)], 1)
    to_far_rows(col_out.at[0], mixed_far, 6)
    for d in range(3):
        for b in range(2):
            block = w_buf.at[:, :, slot((y + 3 - d) % 4, b, c)]
            arrive(block, w_recv.at[4 + 2 * d + b])
            go(block, block, w_send.at[12 + 2 * d + b], w_recv.at[12 + 2 * d + b], core)
    local[3].wait()
    arrive(og_half(x3, 1), o_recv.at[2])
    arrive(og_half(x1, 0), o_recv.at[3])
    arrive(og_half(x2, 0), o_recv.at[4])
    arrive(og_half(x2, 1), o_recv.at[5])
    for b in range(2):
        arrive(w_buf.at[:, :, slot(y, b, 1 - c)], w_recv.at[10 + b])
    for d in range(3):
        for b in range(2):
            arrive(w_buf.at[:, :, slot((y + 3 - d) % 4, b, 1 - c)], w_recv.at[12 + 2 * d + b])

    @pl.loop(0, 3)
    def _(t):
        gm_far[t] = dot(og_buf[wide(t, 256), :], w_buf[1], 1, 1).astype(BF16)

    to_far_columns(gm_far, col_gm.at[1], 7)

    @pl.loop(0, 3)
    def _(t):
        value = dot(og_buf[wide(t, 256), :], w_buf[0], 1, 1)
        total[t] = value
        gm_own[t] = value.astype(BF16)

    to_columns([(gm_own, col_gm.at[0])], 2)
    go(gm_far.at[:, :, row_part], gm_in, z_send.at[1], z_recv.at[1], far)

    arrive(mixed_far.at[:, :, row_part], z_recv.at[0])
    arrive(mixed.at[:, :, col_part], c_recv.at[1])
    arrive(mixed_far.at[:, :, col_part], c_recv.at[6])
    project(x2)
    go(part.at[top, wide(x2, 512)], relay_l, x_send.at[0], x_recv.at[0], right)
    go(part.at[low, wide(x2, 512)], relay_r, x_send.at[1], x_recv.at[1], left)
    project(x1)
    go(part.at[low, wide(x1, 512)], direct_l.at[low], x_send.at[2], x_recv.at[2], right)
    project(x3)
    go(part.at[top, wide(x3, 512)], direct_r.at[top], x_send.at[3], x_recv.at[3], left)

    for a, ref in enumerate((mixed, mixed_far)):
        for group in range(4):

            @pl.loop(0, 2)
            def _(tile):
                rows = wide(tile, 256)
                value = jnp.zeros((256, 512), F32)
                for t in range(3):
                    value += dot(ref[t, :, rows], og_buf[pl.ds(256 * t, 256), pl.ds(512 * group, 512)], 0, 0)
                value = value.astype(BF16)
                for j in range(4):
                    gw_part[j % 2, group, j // 2, a, rows, :] = value[:, 128 * j : 128 * j + 128]

    go(gw_part.at[1 - c], gw_core, g_send.at[0], g_recv.at[0], core)
    arrive(relay_l, x_recv.at[0])
    part[top, wide(x1, 512)] = (part[top, wide(x1, 512)].astype(F32) + relay_l[...].astype(F32)).astype(BF16)
    go(part.at[top, wide(x1, 512)], direct_l.at[top], x_send.at[4], x_recv.at[4], right)
    arrive(relay_r, x_recv.at[1])
    part[low, wide(x3, 512)] = (part[low, wide(x3, 512)].astype(F32) + relay_r[...].astype(F32)).astype(BF16)
    go(part.at[low, wide(x3, 512)], direct_r.at[low], x_send.at[5], x_recv.at[5], left)

    arrive(col_gm.at[0], c_recv.at[2])
    arrive(col_gm.at[1], c_recv.at[7])

    @pl.loop(0, 6)
    def _(i):
        rows = wide(i, 16)
        value = (col_gm[0, rows].astype(F32) + col_gm[1, rows].astype(F32)).astype(BF16)
        col_f[4, wide(i, 256), :] = value.astype(F32).reshape(256, 128)

    columns_of(col_backward)
    for a in range(3):
        narrow(col_f.at[a], col_out.at[a + 1])
    to_rows([(col_out.at[1], gq_ref), (col_out.at[2], gk_ref), (col_out.at[3], gv_ref)], 3)

    arrive(gw_core, g_recv.at[0])
    for d in (1, 2, 3, 0):
        yy = (y + d) % 4

        @pl.loop(0, 2)
        def _(b):
            gw_sum[yy, b] = (gw_part[c, yy, b].astype(F32) + gw_core[yy, b].astype(F32)).astype(BF16)

        if d:
            go(gw_sum.at[yy], gw_ring.at[d - 1], g_send.at[d], g_recv.at[d], rings[d - 1])

    arrive(gm_in, z_recv.at[1])

    @pl.loop(0, 3)
    def _(t):
        gm_row[t] = (total[t, :, row_part] + gm_in[t].astype(F32)).astype(BF16)

    gk_sum[0] = jnp.zeros_like(gk_sum[0])
    gv_sum[0] = jnp.zeros_like(gv_sum[0])

    @pl.loop(0, 2)
    def _(h):
        row_backward(0, h)

    edge_out[0] = (gk_sum[0] * factor).astype(BF16)
    edge_out[1] = gv_sum[0].astype(BF16)
    go(edge_out, edge_in, b_send.at[2], b_recv.at[2], before)

    @pl.loop(2, 6)
    def _(u):
        row_backward(u // 2, u % 2)

    for d in range(3):
        arrive(gw_ring.at[d], g_recv.at[d + 1])

    @pl.loop(0, 2)
    def _(b):
        gw_line[b] = (
            gw_sum[y, b].astype(F32)
            + gw_ring[0, b].astype(F32)
            + gw_ring[1, b].astype(F32)
            + gw_ring[2, b].astype(F32)
        ).astype(BF16)

    ends = []
    for a in range(2):
        for b in range(2):
            owner = device(y, 2 * zh + b, c, x, zh if a == 0 else 1 - zh)
            copy = remote(
                gw_line.at[b, a], gw_last.at[zl], g_send.at[4 + 2 * a + b], g_recv.at[4 + zl], owner
            )
            if a == 0:
                other = zl != 2 * zh + b
                home = pltpu.make_async_copy(gw_line.at[b, a], gw_last.at[zl], g_recv.at[4 + zl])

                @pl.when(other)
                def _():
                    copy.start()

                @pl.when(jnp.logical_not(other))
                def _():
                    home.start()

                ends.append((other, copy))
            else:
                copy.start()
                sends.append(copy)

    project(x)
    arrive(direct_l.at[low], x_recv.at[2])
    arrive(direct_r.at[top], x_recv.at[3])
    arrive(direct_l.at[top], x_recv.at[4])
    arrive(direct_r.at[low], x_recv.at[5])

    @pl.loop(0, 3)
    def _(t):
        rows = wide(t, 256)
        out_ref[t] = (
            part[rows, wide(x, 512)].astype(F32) + direct_l[rows].astype(F32) + direct_r[rows].astype(F32)
        ).astype(BF16)

    arrive(edge_in, b_recv.at[2])

    @pl.loop(0, 3)
    def _(t):
        edge_k = jnp.where(t == 2, edge_in[0].astype(F32), 0.0)
        edge_v = jnp.where(t == 2, edge_in[1].astype(F32), 0.0)
        gk_ref[t, :, row_part] = (gk_sum[t + 1] * factor + edge_k).astype(BF16)
        gv_ref[t, :, row_part] = (gv_sum[t + 1] + edge_v).astype(BF16)

    for n, ref in enumerate((gq_ref, gk_ref, gv_ref)):
        arrive(ref.at[:, :, col_part], c_recv.at[3 + n])
    for z in range(4):
        arrive(gw_last.at[z], g_recv.at[4 + z])
    gw_ref[...] = (
        gw_last[0].astype(F32) + gw_last[1].astype(F32) + gw_last[2].astype(F32) + gw_last[3].astype(F32)
    ).astype(BF16)
    arrive(col_in.at[:, pl.ds(0, 93)], c_send.at[0])
    arrive(col_out.at[0, pl.ds(0, 93)], c_send.at[1])
    arrive(col_gm.at[0, pl.ds(0, 93)], c_send.at[2])
    for n in range(3):
        arrive(col_out.at[n + 1, pl.ds(0, 93)], c_send.at[3 + n])
    arrive(col_out.at[0], c_send.at[6])
    arrive(col_gm.at[0], c_send.at[7])
    for copy in sends:
        copy.wait_send()
    for other, copy in ends:

        @pl.when(other)
        def _():
            copy.wait_send()

    @pl.when(away)
    def _():
        w_away.wait_send()


def per_device(query, key, value, weight_out, output_gradient):
    rows = jax.ShapeDtypeStruct((3, 256, 512), BF16)
    any_space = pl.BlockSpec(memory_space=pl.ANY)
    vmem = pl.BlockSpec(memory_space=pltpu.VMEM)
    dma = pltpu.SemaphoreType.DMA

    def half(*shape):
        return pltpu.VMEM(shape, BF16)

    def full(*shape):
        return pltpu.VMEM(shape, F32)

    output, grad_query, grad_key, grad_value, grad_weight = pl.pallas_call(
        layer_kernel,
        out_shape=(rows, rows, rows, rows, jax.ShapeDtypeStruct((512, 128), BF16)),
        in_specs=[any_space] * 5,
        out_specs=(vmem,) * 5,
        scratch_shapes=[
            half(2, 512, 2048),
            half(768, 2048),
            half(3, 256, 256),
            half(4, 256, 256),
            half(4, 256, 256),
            half(3, 2, 256, 256),
            half(3, 256, 512),
            half(3, 256, 512),
            half(3, 256, 256),
            half(3, 256, 256),
            half(3, 256, 512),
            half(3, 256, 512),
            full(4, 256, 256),
            full(4, 256, 256),
            half(2, 256, 256),
            half(2, 256, 256),
            half(3, 96, 16, 128),
            half(2, 96, 16, 128),
            half(4, 96, 16, 128),
            full(5, 1536, 128),
            half(16, 96, 96),
            half(768, 2048),
            half(384, 512),
            half(384, 512),
            half(768, 512),
            half(768, 512),
            full(3, 256, 512),
            half(2, 4, 2, 2, 512, 128),
            half(4, 2, 2, 512, 128),
            half(4, 2, 2, 512, 128),
            half(3, 2, 2, 512, 128),
            half(2, 2, 512, 128),
            half(4, 512, 128),
            dma((4,)),
            dma((18,)),
            dma((18,)),
            dma((6,)),
            dma((6,)),
            dma((3,)),
            dma((3,)),
            dma((8,)),
            dma((8,)),
            dma((6,)),
            dma((6,)),
            dma((2,)),
            dma((2,)),
            dma((8,)),
            dma((8,)),
        ],
        compiler_params=pltpu.CompilerParams(
            collective_id=0, has_side_effects=True, vmem_limit_bytes=62 * 2**20
        ),
    )(
        query.reshape(3, 256, 512),
        key.reshape(3, 256, 512),
        value.reshape(3, 256, 512),
        weight_out,
        output_gradient,
    )
    return (
        output.reshape(768, 512),
        grad_query.reshape(768, 512),
        grad_key.reshape(768, 512),
        grad_value.reshape(768, 512),
        grad_weight,
    )


def solution(mesh):
    in_specs = (P("seq", "mp"), P("seq", "mp"), P("seq", "mp"), P("mp", "seq"), P("seq", "mp"))
    out_specs = (P("seq", "mp"), P("seq", "mp"), P("seq", "mp"), P("seq", "mp"), P("mp", "seq"))
    return jax.shard_map(
        per_device, mesh=mesh, in_specs=in_specs, out_specs=out_specs, check_vma=False
    )
```

time: 208 us -> 180 us (0.87)
  Pallas kernels: 198 us -> 171 us
    pallas_call x1, Pallas kernels: 198 us -> 171 us  [per_device(): pl.pallas_call(layer_kernel, out_shape=(rows, rows, rows, rows, jax.Shape...]
where the time goes in v3:
time: 180 us; the launch traced here: 179 us
  Pallas kernels  171 us (95%)
  local copies, waits for them, and re-layouts  6.65 us (4%)
    pallas_call x1, Pallas kernels, per_device(): pl.pallas_call(layer_kernel, out_shape=(rows, rows, rows, rows, jax.Shape...  171 us
    unnamed x13, local copies, waits for them, and re-layouts  6.65 us

profile of v3, /device:TPU:96, one launch (start us, length us, event | category | flops | bytes accessed | tf_op | source)
XLA Modules:
  0.0 178.6 jit_solution(340948218261187124)
XLA Ops:
  0.6 171.3 %shard_map.92 = (bf16[3,256,512]{2,1,0:T(8,128)(2,1)}, bf16[3,256,512]{2,1,0:T(8,128)(2,1)}, bf16[3,256,512]{2,1,0:T(8,128)(2,1)}, bf16[3,256,512]{2,1,0:T(8,128)(2,1)}, bf16[512,128]{1,0:T(8,128)(2,1)}) custom-call(bf16[3,256,512]{2,1,0:T(8,128)(2,1)} %bitcast.11, bf16[3,256,512]{2,1,0:T(8,128)(2,1)} %bitcast.12, bf16[3,256,512]{2,1,0:T(8,128)(2,1)} %bitcast.13, ...), custom_call_target="tpu_custom_call" | custom-call | tf_op jit(solution)/shard_map/pallas_call | solution.py:508
  172.0 0.0 copy-start.2
  172.0 2.1 %copy.15 = bf16[768,512]{1,0:T(8,128)(2,1)} copy(bf16[768,512]{1,0:T(8,128)(2,1)} %bitcast.10) | data formatting | bytes 1572864
  174.1 0.0 copy-done.2
  174.1 0.0 copy-start.1
  174.1 0.9 copy.16
  175.0 0.5 copy-done.1
  175.5 0.0 copy-start
  175.5 0.9 copy.17
  176.4 0.5 copy-done
  177.0 0.0 copy-start.3
  177.0 0.9 copy.18
  177.8 0.1 copy-done.3
  178.0 0.7 copy.19
Async XLA Ops:
  172.0 2.1 %copy-start.2 = (bf16[3,256,512]{2,1,0:T(8,128)(2,1)S(1)}, bf16[3,256,512]{2,1,0:T(8,128)(2,1)}, u32[]{:S(2)}) copy-start(bf16[3,256,512]{2,1,0:T(8,128)(2,1)} %get-tuple-element.11) | copy-start | bytes 2359300
  174.1 1.4 copy-start.1
  175.5 1.4 copy-start
  177.0 1.0 copy-start.3

commit v4 on v3

--- a/solution.py
+++ b/solution.py
@@ -46,7 +46,7 @@
     w_buf, og_buf, row_q, row_k, row_v, row_p, gm_own, gm_far, gm_row, gm_in, mixed, mixed_far,
     gk_sum, gv_sum, edge_out, edge_in,
     col_in, col_gm, col_out, col_f, col_p,
-    part, relay_l, relay_r, direct_l, direct_r, total,
+    part, relay_l, relay_r, direct_l, direct_r, total, g_row, result, gw_sumup,
     gw_part, gw_core, gw_sum, gw_ring, gw_line, gw_last,
     own_sem, w_send, w_recv, o_send, o_recv, b_send, b_recv, c_send, c_recv,
     x_send, x_recv, z_send, z_recv, g_send, g_recv,
@@ -204,7 +204,7 @@
         zero = jnp.zeros_like(probs)
         slopes_own, slopes_prior = jnp.where(seen, slopes, zero), jnp.where(seen, zero, slopes)
         probs_own, probs_prior = jnp.where(seen, probs, zero), jnp.where(seen, zero, probs)
-        gq_ref[t, :, head(h)] = (
+        g_row[0, t, :, head(h)] = (
             (dot(slopes_own, row_k[t + 1, :, head(h)], 1, 0) + dot(slopes_prior, row_k[t, :, head(h)], 1, 0))
             * factor
         ).astype(BF16)
@@ -247,10 +247,10 @@
         col_f[2, column(j), :] = dot(probs, grads, 0, 0)
 
     def columns_of(body):
-        @pl.loop(0, 4)
+        @pl.loop(0, 2)
         def _(g):
-            for b in range(4):
-                body(4 * g + b)
+            for b in range(8):
+                body(8 * g + b)
 
     top, low = pl.ds(0, 384), pl.ds(384, 384)
 
@@ -274,15 +274,12 @@
     go(og_half(x3, 0), og_half(x3, 0), o_send.at[4], o_recv.at[4], right)
     arrive(og_half(x1, 1), o_recv.at[1])
     go(og_half(x1, 1), og_half(x1, 1), o_send.at[5], o_recv.at[5], left)
-    for a in range(2):
-        for b in range(2):
+    for b in range(2):
+        for a in range(2):
             arrive(w_buf.at[a, :, slot(y, b, c)], w_recv.at[2 * a + b])
-    for d in range(3):
-        for b in range(2):
-            block = w_buf.at[:, :, slot(y, b, c)]
-            go(block, block, w_send.at[4 + 2 * d + b], w_recv.at[4 + 2 * d + b], rings[d])
-    for b in range(2):
         block = w_buf.at[:, :, slot(y, b, c)]
+        for d in range(2):
+            go(block, block, w_send.at[4 + 2 * d + b], w_recv.at[4 + 2 * d + b], rings[2 * d])
         go(block, block, w_send.at[10 + b], w_recv.at[10 + b], core)
     for b in range(2):
         arrive((row_k, row_v)[b].at[0], b_recv.at[b])
@@ -290,7 +287,19 @@
     @pl.loop(0, 2)
     def _(h):
         row_forward(0, h)
-
+    y1, y2, y3 = (y + 1) % 4, (y + 2) % 4, (y + 3) % 4
+
+    def w_ring(yy, b, index, relay=None):
+        block = w_buf.at[:, :, slot(yy, b, c)]
+        arrive(block, w_recv.at[index])
+        if relay is not None:
+            go(block, block, w_send.at[8 + b], w_recv.at[8 + b], relay)
+        go(block, block, w_send.at[8 + index], w_recv.at[8 + index], core)
+
+    w_ring(y3, 0, 4, rings[0])
+    w_ring(y1, 1, 7, rings[2])
+    w_ring(y3, 1, 5)
+    w_ring(y1, 0, 6)
     arrive(col_in, c_recv.at[0])
     go(mixed.at[:, :, row_part], mixed_far.at[:, :, row_part], z_send.at[0], z_recv.at[0], far)
     for a in range(3):
@@ -299,11 +308,8 @@
     narrow(col_f.at[3], col_out.at[0])
     to_rows([(col_out.at[0], mixed)], 1)
     to_far_rows(col_out.at[0], mixed_far, 6)
-    for d in range(3):
-        for b in range(2):
-            block = w_buf.at[:, :, slot((y + 3 - d) % 4, b, c)]
-            arrive(block, w_recv.at[4 + 2 * d + b])
-            go(block, block, w_send.at[12 + 2 * d + b], w_recv.at[12 + 2 * d + b], core)
+    w_ring(y2, 0, 8)
+    w_ring(y2, 1, 9)
     local[3].wait()
     arrive(og_half(x3, 1), o_recv.at[2])
     arrive(og_half(x1, 0), o_recv.at[3])
@@ -313,7 +319,7 @@
         arrive(w_buf.at[:, :, slot(y, b, 1 - c)], w_recv.at[10 + b])
     for d in range(3):
         for b in range(2):
-            arrive(w_buf.at[:, :, slot((y + 3 - d) % 4, b, 1 - c)], w_recv.at[12 + 2 * d + b])
+            arrive(w_buf.at[:, :, slot((y3, y1, y2)[d], b, 1 - c)], w_recv.at[12 + 2 * d + b])
 
     @pl.loop(0, 3)
     def _(t):
@@ -328,7 +334,6 @@
         gm_own[t] = value.astype(BF16)
 
     to_columns([(gm_own, col_gm.at[0])], 2)
-    go(gm_far.at[:, :, row_part], gm_in, z_send.at[1], z_recv.at[1], far)
 
     arrive(mixed_far.at[:, :, row_part], z_recv.at[0])
     arrive(mixed.at[:, :, col_part], c_recv.at[1])
@@ -355,6 +360,8 @@
                     gw_part[j % 2, group, j // 2, a, rows, :] = value[:, 128 * j : 128 * j + 128]
 
     go(gw_part.at[1 - c], gw_core, g_send.at[0], g_recv.at[0], core)
+    arrive(col_gm.at[0], c_send.at[7])
+    go(gm_far.at[:, :, row_part], gm_in, z_send.at[1], z_recv.at[1], far)
     arrive(relay_l, x_recv.at[0])
     part[top, wide(x1, 512)] = (part[top, wide(x1, 512)].astype(F32) + relay_l[...].astype(F32)).astype(BF16)
     go(part.at[top, wide(x1, 512)], direct_l.at[top], x_send.at[4], x_recv.at[4], right)
@@ -362,6 +369,15 @@
     part[low, wide(x3, 512)] = (part[low, wide(x3, 512)].astype(F32) + relay_r[...].astype(F32)).astype(BF16)
     go(part.at[low, wide(x3, 512)], direct_r.at[low], x_send.at[5], x_recv.at[5], left)
 
+    arrive(gw_core, g_recv.at[0])
+    for b in range(2):
+        for d in (2, 1, 3, 0):
+            yy = (y + d) % 4
+            gw_sum[yy, b] = (gw_part[c, yy, b].astype(F32) + gw_core[yy, b].astype(F32)).astype(BF16)
+            if d:
+                index = 2 * d - 1 + b
+                go(gw_sum.at[yy, b], gw_ring.at[d - 1, b], g_send.at[index], g_recv.at[index], rings[d - 1])
+
     arrive(col_gm.at[0], c_recv.at[2])
     arrive(col_gm.at[1], c_recv.at[7])
 
@@ -376,73 +392,61 @@
         narrow(col_f.at[a], col_out.at[a + 1])
     to_rows([(col_out.at[1], gq_ref), (col_out.at[2], gk_ref), (col_out.at[3], gv_ref)], 3)
 
-    arrive(gw_core, g_recv.at[0])
-    for d in (1, 2, 3, 0):
-        yy = (y + d) % 4
-
-        @pl.loop(0, 2)
-        def _(b):
-            gw_sum[yy, b] = (gw_part[c, yy, b].astype(F32) + gw_core[yy, b].astype(F32)).astype(BF16)
-
-        if d:
-            go(gw_sum.at[yy], gw_ring.at[d - 1], g_send.at[d], g_recv.at[d], rings[d - 1])
-
-    arrive(gm_in, z_recv.at[1])
-
-    @pl.loop(0, 3)
-    def _(t):
-        gm_row[t] = (total[t, :, row_part] + gm_in[t].astype(F32)).astype(BF16)
-
-    gk_sum[0] = jnp.zeros_like(gk_sum[0])
-    gv_sum[0] = jnp.zeros_like(gv_sum[0])
-
-    @pl.loop(0, 2)
-    def _(h):
-        row_backward(0, h)
-
-    edge_out[0] = (gk_sum[0] * factor).astype(BF16)
-    edge_out[1] = gv_sum[0].astype(BF16)
-    go(edge_out, edge_in, b_send.at[2], b_recv.at[2], before)
-
-    @pl.loop(2, 6)
-    def _(u):
-        row_backward(u // 2, u % 2)
-
-    for d in range(3):
-        arrive(gw_ring.at[d], g_recv.at[d + 1])
-
-    @pl.loop(0, 2)
-    def _(b):
+    ends = []
+    def end(b):
+        for d in range(3):
+            arrive(gw_ring.at[d, b], g_recv.at[2 * d + 1 + b])
         gw_line[b] = (
             gw_sum[y, b].astype(F32)
             + gw_ring[0, b].astype(F32)
             + gw_ring[1, b].astype(F32)
             + gw_ring[2, b].astype(F32)
         ).astype(BF16)
-
-    ends = []
-    for a in range(2):
-        for b in range(2):
-            owner = device(y, 2 * zh + b, c, x, zh if a == 0 else 1 - zh)
-            copy = remote(
-                gw_line.at[b, a], gw_last.at[zl], g_send.at[4 + 2 * a + b], g_recv.at[4 + zl], owner
-            )
-            if a == 0:
-                other = zl != 2 * zh + b
-                home = pltpu.make_async_copy(gw_line.at[b, a], gw_last.at[zl], g_recv.at[4 + zl])
-
-                @pl.when(other)
-                def _():
-                    copy.start()
-
-                @pl.when(jnp.logical_not(other))
-                def _():
-                    home.start()
-
-                ends.append((other, copy))
-            else:
-                copy.start()
-                sends.append(copy)
+        away_copy = remote(
+            gw_line.at[b, 1], gw_last.at[zl], g_send.at[7 + b], g_recv.at[7 + zl], device(y, 2 * zh + b, c, x, 1 - zh)
+        )
+        away_copy.start()
+        sends.append(away_copy)
+        other = zl != 2 * zh + b
+        copy = remote(
+            gw_line.at[b, 0], gw_last.at[zl], g_send.at[9 + b], g_recv.at[7 + zl], device(y, 2 * zh + b, c, x, zh)
+        )
+        home = pltpu.make_async_copy(gw_line.at[b, 0], gw_last.at[zl], g_recv.at[7 + zl])
+
+        @pl.when(other)
+        def _():
+            copy.start()
+
+        @pl.when(jnp.logical_not(other))
+        def _():
+            home.start()
+
+        ends.append((other, copy))
+
+    arrive(gm_in, z_recv.at[1])
+
+    @pl.loop(0, 3)
+    def _(t):
+        gm_row[t] = (total[t, :, row_part] + gm_in[t].astype(F32)).astype(BF16)
+
+    gk_sum[0] = jnp.zeros_like(gk_sum[0])
+    gv_sum[0] = jnp.zeros_like(gv_sum[0])
+
+    @pl.loop(0, 2)
+    def _(h):
+        row_backward(0, h)
+
+    edge_out[0] = (gk_sum[0] * factor).astype(BF16)
+    edge_out[1] = gv_sum[0].astype(BF16)
+    go(edge_out, edge_in, b_send.at[2], b_recv.at[2], before)
+    end(0)
+    end(1)
+
+    @pl.loop(2, 6)
+    def _(u):
+        row_backward(u // 2, u % 2)
+
+    keep(g_row.at[0], gq_ref.at[:, :, row_part], own_sem.at[4])
 
     project(x)
     arrive(direct_l.at[low], x_recv.at[2])
@@ -453,33 +457,39 @@
     @pl.loop(0, 3)
     def _(t):
         rows = wide(t, 256)
-        out_ref[t] = (
+        result[t] = (
             part[rows, wide(x, 512)].astype(F32) + direct_l[rows].astype(F32) + direct_r[rows].astype(F32)
         ).astype(BF16)
 
+    keep(result, out_ref, own_sem.at[5])
     arrive(edge_in, b_recv.at[2])
 
     @pl.loop(0, 3)
     def _(t):
         edge_k = jnp.where(t == 2, edge_in[0].astype(F32), 0.0)
         edge_v = jnp.where(t == 2, edge_in[1].astype(F32), 0.0)
-        gk_ref[t, :, row_part] = (gk_sum[t + 1] * factor + edge_k).astype(BF16)
-        gv_ref[t, :, row_part] = (gv_sum[t + 1] + edge_v).astype(BF16)
+        g_row[1, t] = (gk_sum[t + 1] * factor + edge_k).astype(BF16)
+        g_row[2, t] = (gv_sum[t + 1] + edge_v).astype(BF16)
+
+    keep(g_row.at[1], gk_ref.at[:, :, row_part], own_sem.at[6])
+    keep(g_row.at[2], gv_ref.at[:, :, row_part], own_sem.at[7])
 
     for n, ref in enumerate((gq_ref, gk_ref, gv_ref)):
         arrive(ref.at[:, :, col_part], c_recv.at[3 + n])
     for z in range(4):
-        arrive(gw_last.at[z], g_recv.at[4 + z])
-    gw_ref[...] = (
+        arrive(gw_last.at[z], g_recv.at[7 + z])
+    gw_sumup[...] = (
         gw_last[0].astype(F32) + gw_last[1].astype(F32) + gw_last[2].astype(F32) + gw_last[3].astype(F32)
     ).astype(BF16)
+    keep(gw_sumup, gw_ref, own_sem.at[8])
     arrive(col_in.at[:, pl.ds(0, 93)], c_send.at[0])
     arrive(col_out.at[0, pl.ds(0, 93)], c_send.at[1])
     arrive(col_gm.at[0, pl.ds(0, 93)], c_send.at[2])
     for n in range(3):
         arrive(col_out.at[n + 1, pl.ds(0, 93)], c_send.at[3 + n])
     arrive(col_out.at[0], c_send.at[6])
-    arrive(col_gm.at[0], c_send.at[7])
+    for copy in local[4:]:
+        copy.wait()
     for copy in sends:
         copy.wait_send()
     for other, copy in ends:
@@ -493,10 +503,23 @@
         w_away.wait_send()
 
 
+def hand_over(*refs):
+    sources, targets, buffers, in_sem, out_sem = refs[:5], refs[5:10], refs[10:15], refs[15], refs[16]
+    loads = [pltpu.make_async_copy(sources[n], buffers[n], in_sem.at[n]) for n in range(5)]
+    stores = [pltpu.make_async_copy(buffers[n], targets[n], out_sem.at[n]) for n in range(5)]
+    for copy in loads:
+        copy.start()
+    for load, store in zip(loads, stores):
+        load.wait()
+        store.start()
+    for copy in stores:
+        copy.wait()
+
+
 def per_device(query, key, value, weight_out, output_gradient):
     rows = jax.ShapeDtypeStruct((3, 256, 512), BF16)
+    flat = jax.ShapeDtypeStruct((768, 512), BF16)
     any_space = pl.BlockSpec(memory_space=pl.ANY)
-    vmem = pl.BlockSpec(memory_space=pltpu.VMEM)
     dma = pltpu.SemaphoreType.DMA
 
     def half(*shape):
@@ -505,11 +528,11 @@
     def full(*shape):
         return pltpu.VMEM(shape, F32)
 
-    output, grad_query, grad_key, grad_value, grad_weight = pl.pallas_call(
+    results = pl.pallas_call(
         layer_kernel,
         out_shape=(rows, rows, rows, rows, jax.ShapeDtypeStruct((512, 128), BF16)),
         in_specs=[any_space] * 5,
-        out_specs=(vmem,) * 5,
+        out_specs=(any_space,) * 5,
         scratch_shapes=[
             half(2, 512, 2048),
             half(768, 2048),
@@ -538,13 +561,16 @@
             half(768, 512),
             half(768, 512),
             full(3, 256, 512),
+            half(3, 3, 256, 256),
+            half(3, 256, 512),
+            half(512, 128),
             half(2, 4, 2, 2, 512, 128),
             half(4, 2, 2, 512, 128),
             half(4, 2, 2, 512, 128),
             half(3, 2, 2, 512, 128),
             half(2, 2, 512, 128),
             half(4, 512, 128),
-            dma((4,)),
+            dma((9,)),
             dma((18,)),
             dma((18,)),
             dma((6,)),
@@ -557,8 +583,8 @@
             dma((6,)),
             dma((2,)),
             dma((2,)),
-            dma((8,)),
-            dma((8,)),
+            dma((11,)),
+            dma((11,)),
         ],
         compiler_params=pltpu.CompilerParams(
             collective_id=0, has_side_effects=True, vmem_limit_bytes=62 * 2**20
@@ -570,13 +596,13 @@
         weight_out,
         output_gradient,
     )
-    return (
-        output.reshape(768, 512),
-        grad_query.reshape(768, 512),
-        grad_key.reshape(768, 512),
-        grad_value.reshape(768, 512),
-        grad_weight,
-    )
+    return pl.pallas_call(
+        hand_over,
+        out_shape=(flat, flat, flat, flat, jax.ShapeDtypeStruct((512, 128), BF16)),
+        in_specs=[any_space] * 5,
+        out_specs=(any_space,) * 5,
+        scratch_shapes=[half(768, 512)] * 4 + [half(512, 128), dma((5,)), dma((5,))],
+    )(*(array.reshape(-1, array.shape[-1]) for array in results))
 
 
 def solution(mesh):

time: 180 us -> 167 us (0.928)
  local copies, waits for them, and re-layouts: 6.65 us -> 0 us
  Pallas kernels: 171 us -> 166 us
    pallas_call x1, Pallas kernels: 171 us -> 163 us  [per_device(): pl.pallas_call(layer_kernel, out_shape=(rows, rows, rows, rows, jax.Shape...]
    unnamed x13 -> x0, local copies, waits for them, and re-layouts: 6.65 us -> none
    pallas_call x0 -> x1, Pallas kernels: none -> 2.91 us  [per_device(): pl.pallas_call(hand_over, out_shape=(flat, flat, flat, flat, jax.ShapeDty...]
where the time goes in v4:
time: 167 us
  Pallas kernels  166 us (99%)
    pallas_call x1, Pallas kernels, per_device(): pl.pallas_call(layer_kernel, out_shape=(rows, rows, rows, rows, jax.Shape...  163 us

profile of v4, /device:TPU:96, one launch (start us, length us, event | category | flops | bytes accessed | tf_op | source)
XLA Modules:
  0.0 166.7 jit_solution(5001626092589754748)
XLA Ops:
  0.6 163.1 %shard_map.92 = (bf16[3,256,512]{2,1,0:T(8,128)(2,1)}, bf16[3,256,512]{2,1,0:T(8,128)(2,1)}, bf16[3,256,512]{2,1,0:T(8,128)(2,1)}, bf16[3,256,512]{2,1,0:T(8,128)(2,1)}, bf16[512,128]{1,0:T(8,128)(2,1)}) custom-call(bf16[3,256,512]{2,1,0:T(8,128)(2,1)} %bitcast.7, bf16[3,256,512]{2,1,0:T(8,128)(2,1)} %bitcast.8, bf16[3,256,512]{2,1,0:T(8,128)(2,1)} %bitcast.9, ...), custom_call_target="tpu_custom_call" | custom-call | tf_op jit(solution)/shard_map/pallas_call | solution.py:531
  163.7 2.9 %shard_map.93 = (bf16[768,512]{1,0:T(8,128)(2,1)}, bf16[768,512]{1,0:T(8,128)(2,1)}, bf16[768,512]{1,0:T(8,128)(2,1)}, bf16[768,512]{1,0:T(8,128)(2,1)}, bf16[512,128]{1,0:T(8,128)(2,1)}) custom-call(bf16[768,512]{1,0:T(8,128)(2,1)} %bitcast.10, bf16[768,512]{1,0:T(8,128)(2,1)} %bitcast.11, bf16[768,512]{1,0:T(8,128)(2,1)} %bitcast.12, ...), custom_call_target="tpu_custom_call" | custom-call | tf_op jit(solution)/shard_map/pallas_call | solution.py:599

commit v5 on v4

--- a/solution.py
+++ b/solution.py
@@ -553,7 +553,7 @@
             half(3, 96, 16, 128),
             half(2, 96, 16, 128),
             half(4, 96, 16, 128),
-            full(5, 1536, 128),
+            full(5, 1552, 128),
             half(16, 96, 96),
             half(768, 2048),
             half(384, 512),

time: 167 us -> 167 us (level)
  no operation moved by 1% of the time
where the time goes in v5:
time: 167 us
  Pallas kernels  166 us (99%)
    pallas_call x1, Pallas kernels, per_device(): pl.pallas_call(layer_kernel, out_shape=(rows, rows, rows, rows, jax.Shape...  163 us

profile of v5, /device:TPU:96, one launch (start us, length us, event | category | flops | bytes accessed | tf_op | source)
XLA Modules:
  0.0 166.7 jit_solution(11561655487194391586)
XLA Ops:
  0.6 163.1 %shard_map.92 = (bf16[3,256,512]{2,1,0:T(8,128)(2,1)}, bf16[3,256,512]{2,1,0:T(8,128)(2,1)}, bf16[3,256,512]{2,1,0:T(8,128)(2,1)}, bf16[3,256,512]{2,1,0:T(8,128)(2,1)}, bf16[512,128]{1,0:T(8,128)(2,1)}) custom-call(bf16[3,256,512]{2,1,0:T(8,128)(2,1)} %bitcast.7, bf16[3,256,512]{2,1,0:T(8,128)(2,1)} %bitcast.8, bf16[3,256,512]{2,1,0:T(8,128)(2,1)} %bitcast.9, ...), custom_call_target="tpu_custom_call" | custom-call | tf_op jit(solution)/shard_map/pallas_call | solution.py:531
  163.7 2.9 %shard_map.93 = (bf16[768,512]{1,0:T(8,128)(2,1)}, bf16[768,512]{1,0:T(8,128)(2,1)}, bf16[768,512]{1,0:T(8,128)(2,1)}, bf16[768,512]{1,0:T(8,128)(2,1)}, bf16[512,128]{1,0:T(8,128)(2,1)}) custom-call(bf16[768,512]{1,0:T(8,128)(2,1)} %bitcast.10, bf16[768,512]{1,0:T(8,128)(2,1)} %bitcast.11, bf16[768,512]{1,0:T(8,128)(2,1)} %bitcast.12, ...), custom_call_target="tpu_custom_call" | custom-call | tf_op jit(solution)/shard_map/pallas_call | solution.py:599
